TPU v7x, 32 devices: a whole 2x2x4 slice. The times are simulated.
32 devices in a mesh: ctx: 8 (over z, x), tp: 4 (over y, core).
Axes of the slice: x: 2, y: 2, z: 4, core: 2. Of those that a mesh axis runs over, the one named last changes fastest.
Arguments:
- query_in: bfloat16 [12288, 8192], P('ctx', 'tp'), may hold values from -6 to 6
- key_in: bfloat16 [12288, 8192], P('ctx', 'tp'), may hold values from -6 to 6
- value_in: bfloat16 [12288, 8192], P('ctx', 'tp'), may hold values from -6 to 6
- cotangent: bfloat16 [12288, 8192], P('ctx', 'tp'), may hold values from -14 to 14
- filter_taps: float32 [512, 128], P('tp'), may hold values from -1 to 1
Outputs:
- query_grad: bfloat16 [12288, 8192], P('ctx', 'tp')
- key_grad: bfloat16 [12288, 8192], P('ctx', 'tp')
- value_grad: bfloat16 [12288, 8192], P('ctx', 'tp')
- filter_grad: float32 [512, 128], P('tp')
All inputs are finite; a program needn't handle non-finite values.
Results may differ from a plain program's by a relative error of at most 0.0059.
Values may be sent and summed in bfloat16 or wider, within the bound.
No kernel may reach another device: no remote copies, remote signals or barrier semaphores. Data moves between devices by JAX's collectives and lax.ppermute only.
A program may use at most 256 MiB of HBM per device.

v0:
```python
import math

import jax
import jax.numpy as jnp
from jax import lax
from jax.sharding import PartitionSpec as P

clip_ratio = 0.25
epsilon = 1e-06


def from_behind(value, axis, steps):
    count = lax.axis_size(axis)
    initial, last = (max(0, -steps), min(count, count - steps))
    return lax.ppermute(value, axis, [(source, source + steps) for source in range(initial, last)])


def tap_tables(span):
    tap_idx = lax.broadcasted_iota(jnp.int32, (span, span * span), 0)
    flat_idx = lax.broadcasted_iota(jnp.int32, (span, span * span), 1)
    row_idx = flat_idx // span
    col_idx = flat_idx % span
    lower_mask = (row_idx - col_idx == tap_idx).astype(jnp.float32)
    upper_mask = (row_idx - col_idx + span == tap_idx).astype(jnp.float32)
    return (lower_mask, upper_mask)


def to_channels(rows, local_groups, group_size, span):
    count = rows.shape[0] // span
    return rows.reshape(count, span, local_groups, group_size).transpose(2, 3, 0, 1)


def to_tokens(field):
    groups_here, group_size, count, span = field.shape
    return field.transpose(2, 3, 0, 1).reshape(count * span, groups_here * group_size)


def on_device(query_in, key_in, value_in, cotangent, filter_taps):
    high = lax.Precision.HIGHEST
    length, width = query_in.shape
    local_groups, span = filter_taps.shape
    group_size = width // local_groups
    lower_mask, upper_mask = tap_tables(span)
    taps_round = filter_taps.astype(jnp.bfloat16)
    a_low = jnp.dot(taps_round, lower_mask.astype(jnp.bfloat16), preferred_element_type=jnp.float32)
    a_low = a_low.astype(jnp.bfloat16).reshape(local_groups, span, span)
    a_up = jnp.dot(taps_round, upper_mask.astype(jnp.bfloat16), preferred_element_type=jnp.float32)
    a_up = a_up.astype(jnp.bfloat16).reshape(local_groups, span, span)
    mixed_tok = (key_in.astype(jnp.float32) * value_in.astype(jnp.float32)).astype(jnp.bfloat16)
    signal = (cotangent.astype(jnp.float32) * query_in.astype(jnp.float32)).astype(jnp.bfloat16)
    before = from_behind(mixed_tok[length - span :], "ctx", 1)
    after = from_behind(signal[:span], "ctx", -1)
    blocked = to_channels(mixed_tok, local_groups, group_size, span)
    sig_blocks = to_channels(signal, local_groups, group_size, span)
    before_ch = to_channels(before, local_groups, group_size, span)
    after_ch = to_channels(after, local_groups, group_size, span)
    earlier = jnp.concatenate([before_ch, blocked[:, :, :-1]], 2)
    later = jnp.concatenate([sig_blocks[:, :, 1:], after_ch], 2)
    conv = jnp.einsum("gcbj,gij->gcbi", blocked, a_low, preferred_element_type=jnp.float32)
    conv = conv + jnp.einsum("gcbj,gij->gcbi", earlier, a_up, preferred_element_type=jnp.float32)
    conv = to_tokens(conv)
    query_grad = (cotangent.astype(jnp.float32) * conv).astype(jnp.bfloat16)
    back = jnp.einsum("gcbi,gij->gcbj", sig_blocks, a_low, preferred_element_type=jnp.float32)
    back = back + jnp.einsum("gcbi,gij->gcbj", later, a_up, preferred_element_type=jnp.float32)
    back = to_tokens(back)
    key_grad = (back * value_in.astype(jnp.float32)).astype(jnp.bfloat16)
    value_grad = (back * key_in.astype(jnp.float32)).astype(jnp.bfloat16)
    same_block = jnp.einsum(
        "gcbi,gcbj->gij", sig_blocks, blocked, preferred_element_type=jnp.float32
    )
    cross_block = jnp.einsum(
        "gcbi,gcbj->gij", sig_blocks, earlier, preferred_element_type=jnp.float32
    )
    flat_same = same_block.reshape(local_groups, span * span)
    flat_cross = cross_block.reshape(local_groups, span * span)
    local_taps = lax.dot_general(flat_same, lower_mask, (((1,), (1,)), ((), ())), precision=high)
    local_taps = local_taps + lax.dot_general(
        flat_cross, upper_mask, (((1,), (1,)), ((), ())), precision=high
    )
    inverse = 1.0 / math.sqrt(length * lax.axis_size("ctx") * group_size)
    limit = clip_ratio * math.sqrt(local_groups * lax.axis_size("tp") * span)
    total = lax.psum(local_taps, "ctx")
    scaled = total * inverse
    squares = lax.psum(jnp.sum(scaled * scaled), "tp")
    factor = jnp.minimum(1.0, limit / jnp.sqrt(squares + epsilon))
    filter_grad = scaled * factor
    return (query_grad, key_grad, value_grad, filter_grad)


def solution(mesh):
    placed = (P("ctx", "tp"), P("ctx", "tp"), P("ctx", "tp"), P("ctx", "tp"), P("tp", None))
    return jax.shard_map(
        on_device,
        mesh=mesh,
        in_specs=placed,
        out_specs=(P("ctx", "tp"), P("ctx", "tp"), P("ctx", "tp"), P("tp", None)),
        check_vma=False,
    )
```

profile of v0, /device:TPU:0, one launch (start us, length us, event | category | flops | bytes accessed | tf_op | source)
XLA Modules:
  0.0 353.9 jit_solution(36499635420916678)
XLA Ops:
  7.2 8.6 %copy.15 = bf16[1536,2048]{0,1:T(8,128)(2,1)} copy(bf16[1536,2048]{1,0:T(8,128)(2,1)} %param.8) | data formatting | bytes 12582912 | tf_op args[3]
  15.8 8.6 %copy.22 = bf16[1536,2048]{0,1:T(8,128)(2,1)} copy(bf16[1536,2048]{1,0:T(8,128)(2,1)} %param.5) | data formatting | bytes 12582912 | tf_op args[0]
  24.4 6.4 %fusion.1 = bf16[1536,2048]{0,1:T(8,128)(2,1)S(1)} fusion(bf16[1536,2048]{0,1:T(8,128)(2,1)} %copy.15, bf16[1536,2048]{0,1:T(8,128)(2,1)} %copy.22), kind=kLoop, calls=%fused_computation.8 | loop fusion | flops 12582912 | bytes 18874368 | tf_op jit(solution)/shard_map/convert_element_type | solution.py:50
  33.4 3.3 convolution_convert_fusion.1
  39.9 12.2 %reshape.43 = bf16[12,128,128,16]{1,0,3,2:T(8,128)(2,1)} reshape(bf16[1536,2048]{0,1:T(8,128)(2,1)} %copy-done.4) | data formatting | bytes 12582912 | tf_op jit(solution)/shard_map/reshape | solution.py:30
  52.1 6.7 %copy.30 = bf16[128,128,128,1]{2,1,3,0:T(8,128)(2,1)} copy(bf16[128,128,128,1]{0,2,1,3:T(8,128)(2,1)} %bitcast.82) | data formatting | bytes 8388608 | tf_op jit(solution)/shard_map/reshape | solution.py:46
  58.9 6.8 %copy.31 = bf16[128,128,128,1]{2,1,3,0:T(8,128)(2,1)} copy(bf16[128,128,128,1]{0,2,1,3:T(8,128)(2,1)} %bitcast.81) | data formatting | bytes 8388608 | tf_op jit(solution)/shard_map/reshape | solution.py:48
  65.6 6.6 %copy.63 = bf16[12,128,128,16]{1,3,0,2:T(8,128)(2,1)S(1)} copy(bf16[12,128,128,16]{1,0,3,2:T(8,128)(2,1)} %reshape.43) | data formatting | bytes 12582912 | tf_op jit(solution)/shard_map/reshape | solution.py:30
  74.8 3.6 %slice.18 = bf16[128,16,11,128]{3,1,2,0:T(8,128)(2,1)} slice(bf16[128,16,12,128]{3,1,2,0:T(8,128)(2,1)S(1)} %bitcast.68), slice={[0:128], [0:16], [1:12], [0:128]} | slice | bytes 11534336 | tf_op jit(solution)/shard_map/slice | solution.py:58
  78.4 8.6 %copy.16 = bf16[1536,2048]{0,1:T(8,128)(2,1)} copy(bf16[1536,2048]{1,0:T(8,128)(2,1)} %param.6) | data formatting | bytes 12582912 | tf_op args[1]
  87.1 8.8 %copy.17 = bf16[1536,2048]{0,1:T(8,128)(2,1)} copy(bf16[1536,2048]{1,0:T(8,128)(2,1)} %param.7) | data formatting | bytes 12582912 | tf_op args[2]
  95.9 10.5 %fusion.45 = f32[128,16,12,128]{3,1,2,0:T(8,128)} fusion(bf16[128,16,12,128]{3,1,2,0:T(8,128)(2,1)} %bitcast.69, bf16[128,128,128,1]{2,1,3,0:T(8,128)(2,1)} %copy.30), kind=kOutput, calls=%fused_computation.64 | convolution fusion | flops 805306368 | bytes 23068672 | tf_op jit(solution)/shard_map/gcbi,gij->gcbj/dot_general | solution.py:63
  106.4 12.9 %add_bitcast_fusion = f32[12,128,128,16]{1,3,0,2:T(8,128)} fusion(f32[128,16,12,128]{3,1,2,0:T(8,128)} %fusion.45, bf16[128,128,128,1]{2,1,3,0:T(8,128)(2,1)S(1)} %copy-done.3, bf16[128,16,1,128]{3,1,2,0:T(8,128)(2,1)} %bitcast.14, bf16[128,16,11,128]{3,1,2,0:T(8,128)(2,1)} %slice.18), kind=kOutput, calls=%fused_computation.12 | convolution fusion | flops 811597824 | bytes 35651584 | tf_op jit(solution)/shard_map/gcbi,gij->gcbj/dot_general | solution.py:64
  119.3 16.4 %copy.26 = f32[12,128,128,16]{1,0,3,2:T(8,128)} copy(f32[12,128,128,16]{1,3,0,2:T(8,128)} %add_bitcast_fusion) | data formatting | bytes 25165824 | tf_op jit(solution)/shard_map/add | solution.py:64
  135.7 18.5 %fusion.2 = (bf16[1536,2048]{0,1:T(8,128)(2,1)}, bf16[1536,2048]{0,1:T(8,128)(2,1)}, bf16[1536,2048]{0,1:T(8,128)(2,1)S(1)}) fusion(bf16[1536,2048]{0,1:T(8,128)(2,1)} %copy.16, f32[256,8,12,128]{3,2,1,0:T(8,128)} %bitcast.76, bf16[1536,2048]{0,1:T(8,128)(2,1)} %copy.17), kind=kLoop, calls=%fused_computation.9 | loop fusion | flops 25165824 | bytes 44040192 | tf_op jit(solution)/shard_map/convert_element_type | solution.py:67
  157.0 12.2 %reshape.38 = bf16[12,128,128,16]{1,0,3,2:T(8,128)(2,1)} reshape(bf16[1536,2048]{0,1:T(8,128)(2,1)} %copy-done.5) | data formatting | bytes 12582912 | tf_op jit(solution)/shard_map/reshape | solution.py:30
  169.2 6.6 %copy.64 = bf16[12,128,128,16]{1,3,0,2:T(8,128)(2,1)S(1)} copy(bf16[12,128,128,16]{1,0,3,2:T(8,128)(2,1)} %reshape.38) | data formatting | bytes 12582912 | tf_op jit(solution)/shard_map/reshape | solution.py:30
  178.9 3.7 %slice.17 = bf16[128,16,11,128]{3,1,2,0:T(8,128)(2,1)} slice(bf16[128,16,12,128]{3,1,2,0:T(8,128)(2,1)S(1)} %bitcast.78), slice={[0:128], [0:16], [0:11], [0:128]} | slice | bytes 11534336 | tf_op jit(solution)/shard_map/slice | solution.py:57
  182.6 8.7 %fusion.46 = f32[128,128,128,1]{2,1,3,0:T(8,128)} fusion(bf16[128,16,12,128]{3,1,2,0:T(8,128)(2,1)S(1)} %bitcast.72, bf16[128,16,12,128]{3,1,2,0:T(8,128)(2,1)} %bitcast.79), kind=kOutput, calls=%fused_computation.65 | convolution fusion | flops 805306368 | bytes 20971520 | tf_op jit(solution)/shard_map/gcbi,gcbj->gij/dot_general | solution.py:68
  191.3 10.1 %fusion.44 = f32[128,16,12,128]{3,1,2,0:T(8,128)} fusion(bf16[128,16,12,128]{3,1,2,0:T(8,128)(2,1)} %bitcast.80, bf16[128,128,128,1]{2,1,3,0:T(8,128)(2,1)S(1)} %copy-done.1), kind=kOutput, calls=%fused_computation.63 | convolution fusion | flops 805306368 | bytes 23068672 | tf_op jit(solution)/shard_map/gcbj,gij->gcbi/dot_general | solution.py:59
  201.4 8.6 %copy.29 = bf16[1536,2048]{1,0:T(8,128)(2,1)} copy(bf16[1536,2048]{0,1:T(8,128)(2,1)} %get-tuple-element.8) | data formatting | bytes 12582912
  210.0 5.5 %collective-permute-start = (bf16[128,2048]{0,1:T(8,128)(2,1)S(1)}, bf16[128,2048]{0,1:T(8,128)(2,1)S(1)}, u32[]{:S(2)}, u32[]{:S(2)}) collective-permute-start(bf16[128,2048]{0,1:T(8,128)(2,1)S(1)} %slice.16), channel_id=1, source_target_pairs={{0,4},{4,8},{8,12},{12,16},{16,20},{20,24},{24,28},{1,5},{5,9},{9,... | collective-permute-start | bytes 1572872 | tf_op jit(solution)/shard_map/ppermute | solution.py:15
  215.5 8.9 %copy.28 = bf16[1536,2048]{1,0:T(8,128)(2,1)} copy(bf16[1536,2048]{0,1:T(8,128)(2,1)} %get-tuple-element.9) | data formatting | bytes 12582912
  224.4 12.4 %fusion.8 = f32[128,128]{1,0:T(8,128)S(1)} fusion(f32[16,8,128,128]{3,2,1,0:T(8,128)} %bitcast.85, s32[16384]{0:T(1024)S(1)} %get-tuple-element.12, s32[16384]{0:T(1024)S(1)} %get-tuple-element.13, s32[16384]{0:T(1024)S(1)} %get-tuple-element.11, s32[16384]{0:T(1024)S(1)} %get-tuple-element.14, pred[16384]{0:T(1024)(128)(4,1)S(1)} %get-tuple-element.15, ...), kind=kOutput, calls=%fused_computation.17 | convolution fusion | flops 3229614080 | bytes 8749056 | tf_op jit(solution)/shard_map/dot_general | solution.py:76
  236.8 8.4 %fusion.29 = f32[128,128,128,1]{2,1,3,0:T(8,128)} fusion(bf16[128,16,12,128]{3,1,2,0:T(8,128)(2,1)S(1)} %bitcast.75, bf16[128,16,11,128]{3,1,2,0:T(8,128)(2,1)} %slice.17, bf16[128,16,1,128]{3,1,2,0:T(8,128)(2,1)S(1)} %bitcast.83), kind=kOutput, calls=%fused_computation.44 | convolution fusion | flops 808452096 | bytes 20971520 | tf_op jit(solution)/shard_map/gcbi,gcbj->gij/dot_general | solution.py:71
  245.2 13.4 %fusion.30 = f32[128,128]{1,0:T(8,128)} fusion(f32[128,128]{1,0:T(8,128)S(1)} %fusion.8, f32[16,8,128,128]{3,2,1,0:T(8,128)} %bitcast.86, s32[16384]{0:T(1024)S(1)} %get-tuple-element.12, s32[16384]{0:T(1024)S(1)} %get-tuple-element.13, s32[16384]{0:T(1024)S(1)} %get-tuple-element.11, s32[16384]{0:T(1024)S(1)} %get-tuple-element.14, ...), kind=kOutput, calls=%fused_computation.45 | convolution fusion | flops 3231727616 | bytes 8814592 | tf_op jit(solution)/shard_map/dot_general | solution.py:77
  258.6 14.8 %add_bitcast_fusion.1 = f32[12,128,128,16]{1,3,0,2:T(8,128)} fusion(f32[128,16,12,128]{3,1,2,0:T(8,128)} %fusion.44, bf16[128,128,128,1]{2,1,3,0:T(8,128)(2,1)} %copy.31, bf16[128,16,11,128]{3,1,2,0:T(8,128)(2,1)} %slice.17, bf16[128,16,1,128]{3,1,2,0:T(8,128)(2,1)S(1)} %bitcast.84), kind=kOutput, calls=%fused_computation.13 | convolution fusion | flops 811597824 | bytes 35651584 | tf_op jit(solution)/shard_map/gcbj,gij->gcbi/dot_general | solution.py:60
  273.4 16.7 %copy.21 = f32[12,128,128,16]{1,0,3,2:T(8,128)} copy(f32[12,128,128,16]{1,3,0,2:T(8,128)} %add_bitcast_fusion.1) | data formatting | bytes 25165824 | tf_op jit(solution)/shard_map/add | solution.py:60
  290.1 13.9 %fusion = bf16[1536,2048]{0,1:T(8,128)(2,1)} fusion(bf16[1536,2048]{0,1:T(8,128)(2,1)} %copy.15, f32[256,8,12,128]{3,2,1,0:T(8,128)} %bitcast.77), kind=kLoop, calls=%fused_computation.7 | loop fusion | flops 9437184 | bytes 25165824 | tf_op jit(solution)/shard_map/convert_element_type | solution.py:62
  304.0 24.9 %all-reduce.2.cloned.1.call-done = f32[128,128]{1,0:T(8,128)} async-done(((f32[128,128]{1,0:T(8,128)}), f32[128,128]{1,0:T(8,128)}) %all-reduce.2.cloned.1.call-update) | async-done | bytes 65552 | tf_op jit(solution)/shard_map/psum | solution.py:82
  330.4 8.6 %copy.27 = bf16[1536,2048]{1,0:T(8,128)(2,1)} copy(bf16[1536,2048]{0,1:T(8,128)(2,1)} %fusion) | data formatting | bytes 12582912
  339.0 6.3 %psum.15 = f32[]{:T(128)} all-reduce(f32[]{:T(128)} %multiply_reduce_fusion), channel_id=1, replica_groups=mesh['ctx'=8,'tp'=4] {'tp'}, use_global_device_ids=true, to_apply=%region_2.3 | all-reduce | flops 1 | bytes 8 | tf_op jit(solution)/shard_map/psum | solution.py:84
  (39 shorter events, 16.5 us)
Async XLA Ops:
  7.2 321.7 %all-reduce.2.cloned.1.call-start = ((), (), s32[]{:S(2)}) async-start(), calls=%async_computation | async-start | bytes 131072 | tf_op jit(solution)/shard_map/psum | solution.py:82
  24.4 8.9 %copy-start.7 = (f32[128,128]{1,0:T(8,128)S(1)}, f32[128,128]{1,0:T(8,128)}, u32[]{:S(2)}) copy-start(f32[128,128]{1,0:T(8,128)} %param.9) | copy-start | bytes 196612
  30.8 5.9 %copy-start.4 = (bf16[1536,2048]{0,1:T(8,128)(2,1)}, bf16[1536,2048]{0,1:T(8,128)(2,1)S(1)}, u32[]{:S(2)}) copy-start(bf16[1536,2048]{0,1:T(8,128)(2,1)S(1)} %fusion.1) | copy-start | bytes 18874372
  31.8 74.6 %collective-permute-start.1 = (bf16[128,2048]{0,1:T(8,128)(2,1)}, bf16[128,2048]{0,1:T(8,128)(2,1)}, u32[]{:S(2)}, u32[]{:S(2)}) collective-permute-start(bf16[128,2048]{0,1:T(8,128)(2,1)} %slice.19), channel_id=1, source_target_pairs={{4,0},{8,4},{12,8},{16,12},{20,16},{24,20},{28,24},{5,1},{9,5},{13... | collective-permute-start | bytes 1572872 | tf_op jit(solution)/shard_map/ppermute | solution.py:15
  72.2 2.6 copy-start
  95.9 10.5 %copy-start.3 = (bf16[128,128,128,1]{2,1,3,0:T(8,128)(2,1)S(1)}, bf16[128,128,128,1]{2,1,3,0:T(8,128)(2,1)}, u32[]{:S(2)}) copy-start(bf16[128,128,128,1]{2,1,3,0:T(8,128)(2,1)} %copy.31) | copy-start | bytes 12582916
  154.2 2.7 copy-start.5
  175.7 3.2 copy-start.2
  175.8 6.9 %slice-start = ((s8[6291456]{0:T(1024)(128)(4,1)}), s8[4194304]{0:T(1024)(128)(4,1)S(1)}, s32[]{:S(2)}) async-start(s8[6291456]{0:T(1024)(128)(4,1)} %bitcast.70), calls=%async_computation.1 | async-start | bytes 8388608
  178.9 3.7 %slice-start.1 = ((s8[6291456]{0:T(1024)(128)(4,1)}), s8[2097152]{0:T(1024)(128)(4,1)S(1)}, s32[]{:S(2)}) async-start(s8[6291456]{0:T(1024)(128)(4,1)} %bitcast.70), calls=%async_computation.2 | async-start | bytes 4194304
  182.6 8.7 %copy-start.1 = (bf16[128,128,128,1]{2,1,3,0:T(8,128)(2,1)S(1)}, bf16[128,128,128,1]{2,1,3,0:T(8,128)(2,1)}, u32[]{:S(2)}) copy-start(bf16[128,128,128,1]{2,1,3,0:T(8,128)(2,1)} %copy.30) | copy-start | bytes 12582916
  210.0 26.8 %collective-permute-start = (bf16[128,2048]{0,1:T(8,128)(2,1)S(1)}, bf16[128,2048]{0,1:T(8,128)(2,1)S(1)}, u32[]{:S(2)}, u32[]{:S(2)}) collective-permute-start(bf16[128,2048]{0,1:T(8,128)(2,1)S(1)} %slice.16), channel_id=1, source_target_pairs={{0,4},{4,8},{8,12},{12,16},{16,20},{20,24},{24,28},{1,5},{5,9},{9,... | collective-permute-start | bytes 1572872 | tf_op jit(solution)/shard_map/ppermute | solution.py:15
  215.5 21.3 %slice-start.2 = ((s8[6291456]{0:T(1024)(128)(4,1)}), s8[2097152]{0:T(1024)(128)(4,1)S(1)}, s32[]{:S(2)}) async-start(s8[6291456]{0:T(1024)(128)(4,1)} %bitcast.73), calls=%async_computation.3 | async-start | bytes 4194304
  224.4 12.4 %slice-start.3 = ((s8[6291456]{0:T(1024)(128)(4,1)}), s8[4194304]{0:T(1024)(128)(4,1)S(1)}, s32[]{:S(2)}) async-start(s8[6291456]{0:T(1024)(128)(4,1)} %bitcast.73), calls=%async_computation.4 | async-start | bytes 8388608
  330.4 15.6 %copy-start.6 = (f32[128,128]{1,0:T(8,128)S(1)}, f32[128,128]{1,0:T(8,128)}, u32[]{:S(2)}) copy-start(f32[128,128]{1,0:T(8,128)} %all-reduce.2.cloned.1.call-done) | copy-start | bytes 196612
Sparse Core Ops, SparseCore 0:
  258.7 70.1 all-reduce.1
where the time goes:
time: 359 us; the launch traced here: 354 us
  local copies, waits for them, and re-layouts  162 us (45%)
  matrix products  97.6 us (27%)
  other arithmetic  40.9 us (11%)
  waiting for transfers between devices  24.9 us (7%)
  between operations  15.4 us (4%)
  starting transfers between devices  7.02 us (2%)
  blocking collectives  6.27 us (2%)
    unnamed x31, local copies, waits for them, and re-layouts  69.4 us
    reshape x4, local copies, waits for them, and re-layouts, to_channels(): rows.reshape(count, span, local_groups, group_size).transpose(2, 3, 0, 1)  37.5 us
    psum x1, waiting for transfers between devices, on_device(): total = lax.psum(local_taps, 'ctx')  24.9 us
    convert_element_type x1, other arithmetic, on_device(): value_grad = (back * key_in.astype(jnp.float32)).astype(jnp.bfloat16)  18.5 us
    add x1, local copies, waits for them, and re-layouts, on_device(): conv + jnp.einsum('gcbj,gij->gcbi', earlier, a_up, preferred_element_type...  16.7 us
    add x1, local copies, waits for them, and re-layouts, on_device(): back + jnp.einsum('gcbi,gij->gcbj', later, a_up, preferred_element_type=j...  16.4 us
    dot_general x1, matrix products, on_device(): jnp.einsum('gcbj,gij->gcbi', earlier, a_up, preferred_element_type=jnp.fl...  14.8 us
    convert_element_type x1, other arithmetic, on_device(): query_grad = (cotangent.astype(jnp.float32) * conv).astype(jnp.bfloat16)  13.9 us
  transfers between devices with their start and end apart: 3, of which 1 were waited for; matrix products, arithmetic and copies ran while one was open for 39% of the time, Pallas kernels for 0%

commit v1 on v0

v1 whole, which is shorter than its diff:
```python
import math

import jax
import jax.numpy as jnp
from jax import lax
from jax.experimental import pallas as pl
from jax.experimental.pallas import tpu as pltpu
from jax.sharding import PartitionSpec as P

clip_ratio = 0.25
epsilon = 1e-06
LANES = 128
TILE = 16
WIDE = 256
bf16 = jnp.bfloat16
f32 = jnp.float32


def shifted(value, axis, steps):
    count = lax.axis_size(axis)
    first, last = max(0, -steps), min(count, count - steps)
    return lax.ppermute(value, axis, [(source, source + steps) for source in range(first, last)])


def butterfly(value, axis):
    count, step = lax.axis_size(axis), 1
    while step < count:
        value = value + lax.ppermute(value, axis, [(i, i ^ step) for i in range(count)])
        step *= 2
    return value


def toeplitz(tap):
    lane = lax.broadcasted_iota(jnp.int32, (TILE, LANES), 1)
    row = lax.broadcasted_iota(jnp.int32, (TILE, LANES), 0)
    zero = jnp.zeros((TILE, LANES), bf16)
    tap = jnp.broadcast_to(tap.astype(bf16).astype(f32), (TILE, LANES))
    first = pltpu.roll(tap, 0, 1, stride=1, stride_axis=0).astype(bf16)
    upper, lower = [], []
    for a in range(LANES // TILE):
        rows = pltpu.roll(first, a * TILE, 1) if a else first
        keep = lane >= row + a * TILE
        upper.append(jnp.where(keep, rows, zero))
        lower.append(jnp.where(keep, zero, rows))
    return jnp.concatenate(upper, 0), jnp.concatenate(lower, 0)


def diagonal_sums(folded, groups):
    total = jnp.zeros((groups * TILE, LANES), f32)
    source = lax.broadcasted_iota(jnp.int32, (LANES, LANES), 0)
    target = lax.broadcasted_iota(jnp.int32, (LANES, LANES), 1)
    for a in range(0, LANES // TILE, 2):
        left = jnp.concatenate([folded[a], folded[a + 1]], 1)
        right = [((target + TILE * (a + i)) % LANES == source).astype(bf16) for i in range(2)]
        total = total + jnp.dot(left, jnp.concatenate(right, 0), preferred_element_type=f32)
    row = lax.broadcasted_iota(jnp.int32, total.shape, 0)
    for step in (1, 2, 4, 8):
        total = jnp.where(row & step != 0, pltpu.roll(total, LANES - step, 1), total)
    return jnp.sum(total.reshape(groups, TILE, LANES), 1)


def main_body(q_ref, k_ref, v_ref, c_ref, taps_ref, before_ref, after_ref, dq_ref, dk_ref, dv_ref, raw_ref, mt, st, ct, bt, folded):
    length, width = q_ref.shape
    groups = taps_ref.shape[0]
    group = width // groups
    blocks = length // LANES
    lane = lax.broadcasted_iota(jnp.int32, (TILE, LANES), 1)
    row = lax.broadcasted_iota(jnp.int32, (TILE, LANES), 0)
    flat = lambda x: x.reshape(blocks * group, LANES)
    for h in range(width // LANES):
        cols = slice(h * LANES, (h + 1) * LANES)
        mt[h, 0] = before_ref[:, cols].T
        st[h, blocks] = after_ref[:, cols].T
        for b in range(blocks):
            rows = slice(b * LANES, (b + 1) * LANES)
            mt[h, b + 1] = (k_ref[rows, cols] * v_ref[rows, cols]).T
            st[h, b] = (c_ref[rows, cols] * q_ref[rows, cols]).T
        for p in range(LANES // group):
            g = h * (LANES // group) + p
            own = slice(p * group, (p + 1) * group)
            upper, lower = toeplitz(taps_ref[g : g + 1, :])
            mixed = flat(mt[h, 1 : blocks + 1, own, :])
            window = jnp.concatenate([flat(mt[h, :blocks, own, :]), mixed], 1)
            ahead = jnp.concatenate([flat(st[h, :blocks, own, :]), flat(st[h, 1 : blocks + 1, own, :])], 1)
            conv = jnp.dot(window, jnp.concatenate([lower, upper], 0), preferred_element_type=f32)
            back = lax.dot_general(ahead, jnp.concatenate([upper, lower], 1), (((1,), (1,)), ((), ())), preferred_element_type=f32)
            ct[h, :, own, :] = conv.astype(bf16).reshape(blocks, group, LANES)
            bt[h, :, own, :] = back.astype(bf16).reshape(blocks, group, LANES)
            gram = lax.dot_general(mixed, ahead, (((0,), (0,)), ((), ())), preferred_element_type=f32)
            for a in range(LANES // TILE):
                rows = slice(a * TILE, (a + 1) * TILE)
                kept = jnp.where(lane >= row + a * TILE, gram[rows, :LANES], gram[rows, LANES:])
                folded[a, g * TILE : (g + 1) * TILE, :] = kept.astype(bf16)
        for b in range(blocks):
            rows = slice(b * LANES, (b + 1) * LANES)
            dq_ref[rows, cols] = c_ref[rows, cols] * ct[h, b].T
            back = bt[h, b].T
            dk_ref[rows, cols] = v_ref[rows, cols] * back
            dv_ref[rows, cols] = k_ref[rows, cols] * back
    raw_ref[...] = diagonal_sums(folded, groups)


def main_part(q, k, v, c, taps, before, after):
    length, width = q.shape
    local_groups, span = taps.shape
    groups = WIDE * local_groups // width
    blocks, halves = length // LANES, WIDE // LANES
    block = pl.BlockSpec((length, WIDE), lambda i: (0, i))
    halo = pl.BlockSpec((span, WIDE), lambda i: (0, i))
    some = pl.BlockSpec((groups, span), lambda i: (i, 0))
    big = jax.ShapeDtypeStruct((length, width), bf16)
    return pl.pallas_call(
        main_body,
        grid=(width // WIDE,),
        in_specs=[block] * 4 + [some, halo, halo],
        out_specs=[block] * 3 + [some],
        out_shape=[big, big, big, jax.ShapeDtypeStruct((local_groups, span), f32)],
        scratch_shapes=[pltpu.VMEM((halves, blocks + 1, LANES, LANES), bf16)] * 2
        + [pltpu.VMEM((halves, blocks, LANES, LANES), bf16)] * 2
        + [pltpu.VMEM((LANES // TILE, groups * TILE, LANES), bf16)],
        compiler_params=pltpu.CompilerParams(vmem_limit_bytes=48 << 20),
    )(q, k, v, c, taps, before, after)


def on_device(query_in, key_in, value_in, cotangent, filter_taps):
    length, width = query_in.shape
    local_groups, span = filter_taps.shape
    group_size = width // local_groups
    after = shifted(cotangent[:span] * query_in[:span], "ctx", -1)
    before = shifted(key_in[length - span :] * value_in[length - span :], "ctx", 1)
    query_grad, key_grad, value_grad, raw = main_part(query_in, key_in, value_in, cotangent, filter_taps, before, after)
    inverse = 1.0 / math.sqrt(length * lax.axis_size("ctx") * group_size)
    limit = clip_ratio * math.sqrt(local_groups * lax.axis_size("tp") * span)
    scaled = butterfly(raw, "ctx") * inverse
    squares = butterfly(jnp.broadcast_to(jnp.sum(scaled * scaled), (8, LANES)), "tp")[0, 0]
    factor = jnp.minimum(1.0, limit / jnp.sqrt(squares + epsilon))
    return (query_grad, key_grad, value_grad, scaled * factor)


def solution(mesh):
    placed = (P("ctx", "tp"), P("ctx", "tp"), P("ctx", "tp"), P("ctx", "tp"), P("tp", None))
    return jax.shard_map(
        on_device,
        mesh=mesh,
        in_specs=placed,
        out_specs=(P("ctx", "tp"), P("ctx", "tp"), P("ctx", "tp"), P("tp", None)),
        check_vma=False,
    )
```

time: 359 us -> 80.4 us (0.22); the launches traced: 354 us -> 80.1 us
  local copies, waits for them, and re-layouts: 162 us -> 2 us
  matrix products: 97.6 us -> 0 us
  other arithmetic: 40.9 us -> 5.08 us
  Pallas kernels: 0 us -> 25.4 us
  between operations: 15.4 us -> 1.39 us
  starting transfers between devices: 7.02 us -> 16.5 us
  blocking collectives: 6.27 us -> 0 us
  waiting for transfers between devices: 24.9 us -> 29.8 us
    dot_general x10 -> x0, matrix products: 97.6 us -> none  [the longest x1 14.8 us: on_device(): jnp.einsum('gcbj,gij->gcbi', earlier, a_up, preferred_element_type=jnp.fl...]
    unnamed x31 -> x2, local copies, waits for them, and re-layouts: 69.4 us -> 0.84 us
    reshape x6 -> x0, local copies, waits for them, and re-layouts: 51 us -> none  [the longest x4 37.5 us: to_channels(): rows.reshape(count, span, local_groups, group_size).transpose(2, 3, 0, 1)]
    convert_element_type x3 -> x0, other arithmetic: 38.8 us -> none  [the longest x1 18.5 us: on_device(): value_grad = (back * key_in.astype(jnp.float32)).astype(jnp.bfloat16)]
    add x2 -> x0, local copies, waits for them, and re-layouts: 33.1 us -> none  [the longest x1 16.7 us: on_device(): conv + jnp.einsum('gcbj,gij->gcbi', earlier, a_up, preferred_element_type...]
    ppermute x2 -> x7, waiting for transfers between devices: 0.01 us -> 29.8 us  [the longest x2 19.8 us: shifted(): lax.ppermute(value, axis, [(source, source + steps) for source in range(f...]
    pallas_call x0 -> x1, Pallas kernels: none -> 25.4 us  [main_part(): pl.pallas_call(main_body, grid=(width // WIDE,), in_specs=[block] * 4 + [...]
    psum x1 -> x0, waiting for transfers between devices: 24.9 us -> none  [on_device(): total = lax.psum(local_taps, 'ctx')]
  transfers between devices with their start and end apart: 3 -> 7, of which waited for: 1 -> 6; matrix products, arithmetic and copies ran while one was open for 39% -> 2% of each run, Pallas kernels for 0% -> 0%
where the time goes in v1:
time: 80.4 us; the launch traced here: 80.1 us
  waiting for transfers between devices  29.8 us (37%)
  Pallas kernels  25.4 us (32%)
  starting transfers between devices  16.5 us (21%)
  other arithmetic  5.08 us (6%)
  local copies, waits for them, and re-layouts  2 us (2%)
  between operations  1.39 us (2%)
    pallas_call x1, Pallas kernels, main_part(): pl.pallas_call(main_body, grid=(width // WIDE,), in_specs=[block] * 4 + [...  25.4 us
    ppermute x2, waiting for transfers between devices, shifted(): lax.ppermute(value, axis, [(source, source + steps) for source in range(f...  19.8 us
    ppermute x5, starting transfers between devices, butterfly(): lax.ppermute(value, axis, [(i, i ^ step) for i in range(count)])  10.3 us
    ppermute x5, waiting for transfers between devices, butterfly(): lax.ppermute(value, axis, [(i, i ^ step) for i in range(count)])  9.96 us
    ppermute x2, starting transfers between devices, shifted(): lax.ppermute(value, axis, [(source, source + steps) for source in range(f...  6.17 us
  transfers between devices with their start and end apart: 7, of which 6 were waited for; matrix products, arithmetic and copies ran while one was open for 2% of the time, Pallas kernels for 0%

profile of v1, /device:TPU:0, one launch (start us, length us, event | category | flops | bytes accessed | tf_op | source)
XLA Modules:
  0.0 80.1 jit_solution(4291276726864325920)
XLA Ops:
  0.6 1.3 %slice_multiply_fusion.1 = bf16[128,2048]{1,0:T(8,128)(2,1)S(1)} fusion(bf16[1536,2048]{1,0:T(8,128)(2,1)} %v_ref.1, bf16[1536,2048]{1,0:T(8,128)(2,1)} %k_ref.1), kind=kLoop, calls=%fused_computation.1 | loop fusion | flops 262144 | bytes 1572864 | tf_op jit(solution)/shard_map/mul | solution.py:130
  1.9 4.9 %collective-permute-start = (bf16[128,2048]{1,0:T(8,128)(2,1)S(1)}, bf16[128,2048]{1,0:T(8,128)(2,1)S(1)}, u32[]{:S(2)}, u32[]{:S(2)}) collective-permute-start(bf16[128,2048]{1,0:T(8,128)(2,1)S(1)} %slice_multiply_fusion.1), channel_id=1, source_target_pairs={{0,4},{4,8},{8,12},{12,16},{16,20},{20,24},{24,28},{1,5},{5,9},{9,... | collective-permute-start | bytes 1572872 | tf_op jit(solution)/shard_map/ppermute | solution.py:22
  6.8 1.3 %slice_multiply_fusion = bf16[128,2048]{1,0:T(8,128)(2,1)S(1)} fusion(bf16[1536,2048]{1,0:T(8,128)(2,1)} %q_ref.1, bf16[1536,2048]{1,0:T(8,128)(2,1)} %c_ref.1), kind=kLoop, calls=%fused_computation | loop fusion | flops 262144 | bytes 1572864 | tf_op jit(solution)/shard_map/mul | solution.py:129
  8.0 1.3 %collective-permute-start.1 = (bf16[128,2048]{1,0:T(8,128)(2,1)S(1)}, bf16[128,2048]{1,0:T(8,128)(2,1)S(1)}, u32[]{:S(2)}, u32[]{:S(2)}) collective-permute-start(bf16[128,2048]{1,0:T(8,128)(2,1)S(1)} %slice_multiply_fusion), channel_id=1, source_target_pairs={{4,0},{8,4},{12,8},{16,12},{20,16},{24,20},{28,24},{5,1},{9,5},{13... | collective-permute-start | bytes 1572872 | tf_op jit(solution)/shard_map/ppermute | solution.py:22
  9.3 19.8 %collective-permute-done.before_ref = bf16[128,2048]{1,0:T(8,128)(2,1)S(1)} collective-permute-done((bf16[128,2048]{1,0:T(8,128)(2,1)S(1)}, bf16[128,2048]{1,0:T(8,128)(2,1)S(1)}, u32[]{:S(2)}, u32[]{:S(2)}) %collective-permute-start) | collective-permute-done | bytes 524320 | tf_op jit(solution)/shard_map/ppermute | solution.py:22
  29.1 0.0 collective-permute-done.1.after_ref
  29.1 0.0 copy-start
  29.1 0.8 %copy-done = f32[128,128]{1,0:T(8,128)S(1)} copy-done((f32[128,128]{1,0:T(8,128)S(1)}, f32[128,128]{1,0:T(8,128)}, u32[]{:S(2)}) %copy-start) | copy-done | bytes 65560
  30.0 25.4 %shard_map.84 = (bf16[1536,2048]{1,0:T(8,128)(2,1)}, bf16[1536,2048]{1,0:T(8,128)(2,1)}, bf16[1536,2048]{1,0:T(8,128)(2,1)}, f32[128,128]{1,0:T(8,128)S(1)}) custom-call(bf16[1536,2048]{1,0:T(8,128)(2,1)} %q_ref.1, bf16[1536,2048]{1,0:T(8,128)(2,1)} %k_ref.1, bf16[1536,2048]{1,0:T(8,128)(2,1)} %v_ref.1, bf16[1536,2048]{1,0:T(8,128)(2,1)} %c_ref.1, ...), custom_call_target="tpu_custom_call" | custom-call | tf_op jit(solution)/shard_map/pallas_call | solution.py:112
  55.3 2.5 %collective-permute-start.2 = (f32[128,128]{1,0:T(8,128)S(1)}, f32[128,128]{1,0:T(8,128)S(1)}, u32[]{:S(2)}, u32[]{:S(2)}) collective-permute-start(f32[128,128]{1,0:T(8,128)S(1)} %get-tuple-element.11), channel_id=1, source_target_pairs={{0,4},{4,0},{8,12},{12,8},{16,20},{20,16},{24,28},{28,24},{1,5},{5... | collective-permute-start | bytes 196616 | tf_op jit(solution)/shard_map/ppermute | solution.py:28
  57.8 2.2 %collective-permute-done.2 = f32[128,128]{1,0:T(8,128)S(1)} collective-permute-done((f32[128,128]{1,0:T(8,128)S(1)}, f32[128,128]{1,0:T(8,128)S(1)}, u32[]{:S(2)}, u32[]{:S(2)}) %collective-permute-start.2) | collective-permute-done | bytes 65568 | tf_op jit(solution)/shard_map/ppermute | solution.py:28
  60.1 3.1 %collective-permute-start.3 = (f32[128,128]{1,0:T(8,128)S(1)}, f32[128,128]{1,0:T(8,128)S(1)}, u32[]{:S(2)}, u32[]{:S(2)}) collective-permute-start(f32[128,128]{1,0:T(8,128)S(1)} %add.19), channel_id=1, source_target_pairs={{0,8},{4,12},{8,0},{12,4},{16,24},{20,28},{24,16},{28,20},{1,9},{5... | collective-permute-start | bytes 196616 | tf_op jit(solution)/shard_map/ppermute | solution.py:28
  63.2 2.2 %collective-permute-done.3 = f32[128,128]{1,0:T(8,128)S(1)} collective-permute-done((f32[128,128]{1,0:T(8,128)S(1)}, f32[128,128]{1,0:T(8,128)S(1)}, u32[]{:S(2)}, u32[]{:S(2)}) %collective-permute-start.3) | collective-permute-done | bytes 65568 | tf_op jit(solution)/shard_map/ppermute | solution.py:28
  65.4 3.1 %collective-permute-start.4 = (f32[128,128]{1,0:T(8,128)S(1)}, f32[128,128]{1,0:T(8,128)S(1)}, u32[]{:S(2)}, u32[]{:S(2)}) collective-permute-start(f32[128,128]{1,0:T(8,128)S(1)} %add.20), channel_id=1, source_target_pairs={{0,16},{4,20},{8,24},{12,28},{16,0},{20,4},{24,8},{28,12},{1,17},{... | collective-permute-start | bytes 196616 | tf_op jit(solution)/shard_map/ppermute | solution.py:28
  68.5 2.2 %collective-permute-done.4 = f32[128,128]{1,0:T(8,128)S(1)} collective-permute-done((f32[128,128]{1,0:T(8,128)S(1)}, f32[128,128]{1,0:T(8,128)S(1)}, u32[]{:S(2)}, u32[]{:S(2)}) %collective-permute-start.4) | collective-permute-done | bytes 65568 | tf_op jit(solution)/shard_map/ppermute | solution.py:28
  70.7 0.6 multiply_reduce_fusion
  71.4 0.6 broadcast_in_dim.3
  72.0 0.1 collective-permute-start.5
  72.1 1.2 %collective-permute-done.5 = f32[8,128]{1,0:T(8,128)S(1)} collective-permute-done((f32[8,128]{1,0:T(8,128)S(1)}, f32[8,128]{1,0:T(8,128)S(1)}, u32[]{:S(2)}, u32[]{:S(2)}) %collective-permute-start.5) | collective-permute-done | bytes 4128 | tf_op jit(solution)/shard_map/ppermute | solution.py:28
  73.2 0.6 broadcast_add_fusion
  73.9 1.6 %collective-permute-start.6 = (f32[8,128]{1,0:T(8,128)S(1)}, f32[8,128]{1,0:T(8,128)S(1)}, u32[]{:S(2)}, u32[]{:S(2)}) collective-permute-start(f32[8,128]{1,0:T(8,128)S(1)} %broadcast_add_fusion), channel_id=1, source_target_pairs={{0,2},{1,3},{2,0},{3,1},{4,6},{5,7},{6,4},{7,5},{8,10},{9,11},{10,... | collective-permute-start | bytes 12296 | tf_op jit(solution)/shard_map/ppermute | solution.py:28
  75.5 2.1 %collective-permute-done.6 = f32[8,128]{1,0:T(8,128)S(1)} collective-permute-done((f32[8,128]{1,0:T(8,128)S(1)}, f32[8,128]{1,0:T(8,128)S(1)}, u32[]{:S(2)}, u32[]{:S(2)}) %collective-permute-start.6) | collective-permute-done | bytes 4128 | tf_op jit(solution)/shard_map/ppermute | solution.py:28
  77.6 0.6 fusion
  78.2 0.5 slice.19
  79.4 0.6 broadcast_multiply_fusion
  (2 shorter events, 0.0 us)
Async XLA Ops:
  1.9 27.2 %collective-permute-start = (bf16[128,2048]{1,0:T(8,128)(2,1)S(1)}, bf16[128,2048]{1,0:T(8,128)(2,1)S(1)}, u32[]{:S(2)}, u32[]{:S(2)}) collective-permute-start(bf16[128,2048]{1,0:T(8,128)(2,1)S(1)} %slice_multiply_fusion.1), channel_id=1, source_target_pairs={{0,4},{4,8},{8,12},{12,16},{16,20},{20,24},{24,28},{1,5},{5,9},{9,... | collective-permute-start | bytes 1572872 | tf_op jit(solution)/shard_map/ppermute | solution.py:22
  8.0 21.1 %collective-permute-start.1 = (bf16[128,2048]{1,0:T(8,128)(2,1)S(1)}, bf16[128,2048]{1,0:T(8,128)(2,1)S(1)}, u32[]{:S(2)}, u32[]{:S(2)}) collective-permute-start(bf16[128,2048]{1,0:T(8,128)(2,1)S(1)} %slice_multiply_fusion), channel_id=1, source_target_pairs={{4,0},{8,4},{12,8},{16,12},{20,16},{24,20},{28,24},{5,1},{9,5},{13... | collective-permute-start | bytes 1572872 | tf_op jit(solution)/shard_map/ppermute | solution.py:22
  29.1 0.8 %copy-start = (f32[128,128]{1,0:T(8,128)S(1)}, f32[128,128]{1,0:T(8,128)}, u32[]{:S(2)}) copy-start(f32[128,128]{1,0:T(8,128)} %taps_ref.1) | copy-start | bytes 196612
  55.3 4.7 %collective-permute-start.2 = (f32[128,128]{1,0:T(8,128)S(1)}, f32[128,128]{1,0:T(8,128)S(1)}, u32[]{:S(2)}, u32[]{:S(2)}) collective-permute-start(f32[128,128]{1,0:T(8,128)S(1)} %get-tuple-element.11), channel_id=1, source_target_pairs={{0,4},{4,0},{8,12},{12,8},{16,20},{20,16},{24,28},{28,24},{1,5},{5... | collective-permute-start | bytes 196616 | tf_op jit(solution)/shard_map/ppermute | solution.py:28
  60.1 5.3 %collective-permute-start.3 = (f32[128,128]{1,0:T(8,128)S(1)}, f32[128,128]{1,0:T(8,128)S(1)}, u32[]{:S(2)}, u32[]{:S(2)}) collective-permute-start(f32[128,128]{1,0:T(8,128)S(1)} %add.19), channel_id=1, source_target_pairs={{0,8},{4,12},{8,0},{12,4},{16,24},{20,28},{24,16},{28,20},{1,9},{5... | collective-permute-start | bytes 196616 | tf_op jit(solution)/shard_map/ppermute | solution.py:28
  65.4 5.3 %collective-permute-start.4 = (f32[128,128]{1,0:T(8,128)S(1)}, f32[128,128]{1,0:T(8,128)S(1)}, u32[]{:S(2)}, u32[]{:S(2)}) collective-permute-start(f32[128,128]{1,0:T(8,128)S(1)} %add.20), channel_id=1, source_target_pairs={{0,16},{4,20},{8,24},{12,28},{16,0},{20,4},{24,8},{28,12},{1,17},{... | collective-permute-start | bytes 196616 | tf_op jit(solution)/shard_map/ppermute | solution.py:28
  72.0 1.2 %collective-permute-start.5 = (f32[8,128]{1,0:T(8,128)S(1)}, f32[8,128]{1,0:T(8,128)S(1)}, u32[]{:S(2)}, u32[]{:S(2)}) collective-permute-start(f32[8,128]{1,0:T(8,128)S(1)} %broadcast_in_dim.3), channel_id=1, source_target_pairs={{0,1},{1,0},{2,3},{3,2},{4,5},{5,4},{6,7},{7,6},{8,9},{9,8},{10,11... | collective-permute-start | bytes 12296 | tf_op jit(solution)/shard_map/ppermute | solution.py:28
  73.9 3.7 %collective-permute-start.6 = (f32[8,128]{1,0:T(8,128)S(1)}, f32[8,128]{1,0:T(8,128)S(1)}, u32[]{:S(2)}, u32[]{:S(2)}) collective-permute-start(f32[8,128]{1,0:T(8,128)S(1)} %broadcast_add_fusion), channel_id=1, source_target_pairs={{0,2},{1,3},{2,0},{3,1},{4,6},{5,7},{6,4},{7,5},{8,10},{9,11},{10,... | collective-permute-start | bytes 12296 | tf_op jit(solution)/shard_map/ppermute | solution.py:28

commit v2 on v1

--- a/solution.py
+++ b/solution.py
@@ -12,6 +12,8 @@
 LANES = 128
 TILE = 16
 WIDE = 256
+VMEM = 60 << 20
+EDGE_VMEM = 61 << 20
 bf16 = jnp.bfloat16
 f32 = jnp.float32
 
@@ -22,12 +24,32 @@
     return lax.ppermute(value, axis, [(source, source + steps) for source in range(first, last)])
 
 
-def butterfly(value, axis):
-    count, step = lax.axis_size(axis), 1
-    while step < count:
-        value = value + lax.ppermute(value, axis, [(i, i ^ step) for i in range(count)])
-        step *= 2
-    return value
+def partners(value, masks):
+    across, along = lax.axis_size("ctx"), lax.axis_size("tp")
+    numbers = range(across * along)
+    return [lax.ppermute(value, ("ctx", "tp"), [(i, i ^ (c * along + t)) for i in numbers]) for c, t in masks]
+
+
+def summed(value, received):
+    if len(received) == 1:
+        return value + received[0]
+    return (value + received[0]) + (received[1] + received[2])
+
+
+def rounds(bits):
+    out = []
+    while bits:
+        a, b, bits = bits[0], bits[1] if len(bits) > 1 else 0, bits[2:]
+        out.append([a, b, a ^ b] if b else [a])
+    return out
+
+
+def powers(lowest, count):
+    out = []
+    while lowest < count:
+        out.append(lowest)
+        lowest *= 2
+    return out
 
 
 def toeplitz(tap):
@@ -51,15 +73,16 @@
     target = lax.broadcasted_iota(jnp.int32, (LANES, LANES), 1)
     for a in range(0, LANES // TILE, 2):
         left = jnp.concatenate([folded[a], folded[a + 1]], 1)
-        right = [((target + TILE * (a + i)) % LANES == source).astype(bf16) for i in range(2)]
+        right = [((source + target) % LANES == TILE * (a + i)).astype(bf16) for i in range(2)]
         total = total + jnp.dot(left, jnp.concatenate(right, 0), preferred_element_type=f32)
-    row = lax.broadcasted_iota(jnp.int32, total.shape, 0)
-    for step in (1, 2, 4, 8):
-        total = jnp.where(row & step != 0, pltpu.roll(total, LANES - step, 1), total)
-    return jnp.sum(total.reshape(groups, TILE, LANES), 1)
-
-
-def main_body(q_ref, k_ref, v_ref, c_ref, taps_ref, before_ref, after_ref, dq_ref, dk_ref, dv_ref, raw_ref, mt, st, ct, bt, folded):
+    sums = []
+    for g in range(groups):
+        part = pltpu.roll(total[g * TILE : (g + 1) * TILE], 0, 1, stride=1, stride_axis=0)
+        sums.append(jnp.sum(part, 0, keepdims=True))
+    return jnp.concatenate(sums, 0)
+
+
+def main_body(q_ref, k_ref, v_ref, c_ref, taps_ref, dq_ref, dk_ref, dv_ref, folded, first_ref, last_ref, lower_ref, mt, st, ct, bt):
     length, width = q_ref.shape
     groups = taps_ref.shape[0]
     group = width // groups
@@ -69,8 +92,8 @@
     flat = lambda x: x.reshape(blocks * group, LANES)
     for h in range(width // LANES):
         cols = slice(h * LANES, (h + 1) * LANES)
-        mt[h, 0] = before_ref[:, cols].T
-        st[h, blocks] = after_ref[:, cols].T
+        mt[h, 0] = jnp.zeros((LANES, LANES), bf16)
+        st[h, blocks] = jnp.zeros((LANES, LANES), bf16)
         for b in range(blocks):
             rows = slice(b * LANES, (b + 1) * LANES)
             mt[h, b + 1] = (k_ref[rows, cols] * v_ref[rows, cols]).T
@@ -79,6 +102,7 @@
             g = h * (LANES // group) + p
             own = slice(p * group, (p + 1) * group)
             upper, lower = toeplitz(taps_ref[g : g + 1, :])
+            lower_ref[g] = lower
             mixed = flat(mt[h, 1 : blocks + 1, own, :])
             window = jnp.concatenate([flat(mt[h, :blocks, own, :]), mixed], 1)
             ahead = jnp.concatenate([flat(st[h, :blocks, own, :]), flat(st[h, 1 : blocks + 1, own, :])], 1)
@@ -93,14 +117,18 @@
                 folded[a, g * TILE : (g + 1) * TILE, :] = kept.astype(bf16)
         for b in range(blocks):
             rows = slice(b * LANES, (b + 1) * LANES)
-            dq_ref[rows, cols] = c_ref[rows, cols] * ct[h, b].T
+            conv = ct[h, b].T
             back = bt[h, b].T
+            if b == 0:
+                first_ref[:, cols] = conv
+            if b == blocks - 1:
+                last_ref[:, cols] = back
+            dq_ref[rows, cols] = c_ref[rows, cols] * conv
             dk_ref[rows, cols] = v_ref[rows, cols] * back
             dv_ref[rows, cols] = k_ref[rows, cols] * back
-    raw_ref[...] = diagonal_sums(folded, groups)
-
-
-def main_part(q, k, v, c, taps, before, after):
+
+
+def main_part(q, k, v, c, taps):
     length, width = q.shape
     local_groups, span = taps.shape
     groups = WIDE * local_groups // width
@@ -109,32 +137,163 @@
     halo = pl.BlockSpec((span, WIDE), lambda i: (0, i))
     some = pl.BlockSpec((groups, span), lambda i: (i, 0))
     big = jax.ShapeDtypeStruct((length, width), bf16)
+    edge = jax.ShapeDtypeStruct((span, width), bf16)
     return pl.pallas_call(
         main_body,
         grid=(width // WIDE,),
-        in_specs=[block] * 4 + [some, halo, halo],
-        out_specs=[block] * 3 + [some],
-        out_shape=[big, big, big, jax.ShapeDtypeStruct((local_groups, span), f32)],
+        in_specs=[block] * 4 + [some],
+        out_specs=[block] * 3 + [pl.BlockSpec((span // TILE, groups * TILE, span), lambda i: (0, i, 0)), halo, halo, pl.BlockSpec((groups, span, span), lambda i: (i, 0, 0))],
+        out_shape=[big, big, big, jax.ShapeDtypeStruct((span // TILE, local_groups * TILE, span), bf16), edge, edge, jax.ShapeDtypeStruct((local_groups, span, span), bf16)],
         scratch_shapes=[pltpu.VMEM((halves, blocks + 1, LANES, LANES), bf16)] * 2
-        + [pltpu.VMEM((halves, blocks, LANES, LANES), bf16)] * 2
-        + [pltpu.VMEM((LANES // TILE, groups * TILE, LANES), bf16)],
-        compiler_params=pltpu.CompilerParams(vmem_limit_bytes=48 << 20),
-    )(q, k, v, c, taps, before, after)
+        + [pltpu.VMEM((halves, blocks, LANES, LANES), bf16)] * 2,
+        compiler_params=pltpu.CompilerParams(vmem_limit_bytes=VMEM),
+        cost_estimate=pl.CostEstimate(flops=12 * length * width * LANES, bytes_accessed=14 * length * width, transcendentals=0),
+    )(q, k, v, c, taps)
+
+
+def edge_raw_body(k_ref, v_ref, after_ref, inner_ref, out_ref, folded):
+    width = k_ref.shape[1]
+    groups = out_ref.shape[0]
+    group = width // groups
+    lane = lax.broadcasted_iota(jnp.int32, (TILE, LANES), 1)
+    row = lax.broadcasted_iota(jnp.int32, (TILE, LANES), 0)
+    per = LANES // group
+    zero = jnp.zeros((TILE, LANES), bf16)
+    for h in range(width // LANES):
+        cols = slice(h * LANES, (h + 1) * LANES)
+        mixed = k_ref[:, cols] * v_ref[:, cols]
+        ahead = after_ref[:, cols].T
+        empty = jnp.zeros((group, LANES), bf16)
+        for p in range(0, per, 2):
+            pick = lambda n: jnp.concatenate([ahead[i * group : (i + 1) * group] if i == n else empty for i in range(per)], 0)
+            gram = jnp.dot(mixed, jnp.concatenate([pick(p), pick(p + 1)], 1), preferred_element_type=f32)
+            for n in range(2):
+                g = h * per + p + n
+                at = slice(g * TILE, (g + 1) * TILE)
+                for a in range(LANES // TILE):
+                    part = gram[a * TILE : (a + 1) * TILE, n * LANES : (n + 1) * LANES].astype(bf16)
+                    folded[a, at, :] = inner_ref[a, at, :] + jnp.where(lane < row + a * TILE, part, zero)
+    out_ref[...] = diagonal_sums(folded, groups)
+
+
+def edge_raw(k, v, after, inner, wide):
+    length, width = k.shape
+    span = inner.shape[2]
+    local_groups = inner.shape[1] // TILE
+    groups = wide * local_groups // width
+    tail = pl.BlockSpec((span, wide), lambda i: (length // span - 1, i))
+    halo = pl.BlockSpec((span, wide), lambda i: (0, i))
+    return pl.pallas_call(
+        edge_raw_body,
+        grid=(width // wide,),
+        in_specs=[tail, tail, halo, pl.BlockSpec((span // TILE, groups * TILE, span), lambda i: (0, i, 0))],
+        out_specs=pl.BlockSpec((groups, span), lambda i: (i, 0)),
+        out_shape=jax.ShapeDtypeStruct((local_groups, span), f32),
+        scratch_shapes=[pltpu.VMEM((LANES // TILE, groups * TILE, LANES), bf16)],
+        compiler_params=pltpu.CompilerParams(vmem_limit_bytes=EDGE_VMEM),
+        cost_estimate=pl.CostEstimate(flops=2 * span * span * width, bytes_accessed=14 * span * width, transcendentals=0),
+    )(k, v, after, inner)
+
+
+def edge_terms(halo_ref, lower_ref, h, side):
+    group = halo_ref.shape[1] // lower_ref.shape[0]
+    per = LANES // group
+    far = halo_ref[:, h * LANES : (h + 1) * LANES].T
+    parts = []
+    for p in range(per):
+        dims = (((1,), (side,)), ((), ()))
+        parts.append(lax.dot_general(far[p * group : (p + 1) * group], lower_ref[h * per + p], dims, preferred_element_type=f32))
+    return jnp.concatenate(parts, 0).astype(bf16).T.astype(f32)
+
+
+def edge_query_body(before_ref, first_ref, lower_ref, c_ref, dq_in, dq_ref):
+    for h in range(c_ref.shape[1] // LANES):
+        cols = slice(h * LANES, (h + 1) * LANES)
+        conv = first_ref[:, cols].astype(f32) + edge_terms(before_ref, lower_ref, h, 0)
+        dq_ref[:, cols] = c_ref[:, cols] * conv.astype(bf16)
+
+
+def edge_key_body(after_ref, last_ref, lower_ref, k_ref, v_ref, dk_in, dv_in, dk_ref, dv_ref):
+    for h in range(k_ref.shape[1] // LANES):
+        cols = slice(h * LANES, (h + 1) * LANES)
+        back = (last_ref[:, cols].astype(f32) + edge_terms(after_ref, lower_ref, h, 1)).astype(bf16)
+        dk_ref[:, cols] = v_ref[:, cols] * back
+        dv_ref[:, cols] = k_ref[:, cols] * back
+
+
+def edge_outputs(body, tail, halo, inner, lower, factors, grads, wide):
+    length, width = grads[0].shape
+    span = lower.shape[1]
+    place = length // span - 1 if tail else 0
+    head = pl.BlockSpec((span, wide), lambda i: (0, i))
+    edge = pl.BlockSpec((span, wide), lambda i: (place, i))
+    some = pl.BlockSpec((wide * lower.shape[0] // width, span, span), lambda i: (i, 0, 0))
+    count, ahead = len(grads), 3 + len(factors)
+    return pl.pallas_call(
+        body,
+        grid=(width // wide,),
+        in_specs=[head, head, some] + [edge] * len(factors) + [pl.BlockSpec(memory_space=pl.ANY)] * count,
+        out_specs=[edge] * count,
+        out_shape=[jax.ShapeDtypeStruct(g.shape, bf16) for g in grads],
+        input_output_aliases={ahead + i: i for i in range(count)},
+        compiler_params=pltpu.CompilerParams(vmem_limit_bytes=EDGE_VMEM),
+        cost_estimate=pl.CostEstimate(flops=2 * span * span * width, bytes_accessed=12 * span * width, transcendentals=0),
+    )(halo, inner, lower, *factors, *grads)
+
+
+def norm_body(inverse, own_ref, *refs):
+    out_ref, squares_ref = refs[-2:]
+    own = (own_ref[...] + refs[0][...]) * inverse
+    total = jnp.sum(own * own)
+    if len(refs) == 5:
+        other = (refs[1][...] + refs[2][...]) * inverse
+        total = total + jnp.sum(other * other)
+    out_ref[...] = own
+    squares_ref[...] = jnp.full(squares_ref.shape, total, f32)
+
+
+def scale_body(limit, scaled_ref, *refs):
+    out_ref = refs[-1]
+    squares = refs[0][...]
+    for ref in refs[1:-1]:
+        squares = squares + ref[...]
+    factor = jnp.minimum(1.0, limit / jnp.sqrt(squares[:1] + epsilon))
+    flip = (lax.broadcasted_iota(jnp.int32, (LANES, LANES), 0) + lax.broadcasted_iota(jnp.int32, (LANES, LANES), 1)) % LANES == 0
+    out_ref[...] = jnp.dot(scaled_ref[...] * factor, flip.astype(f32), precision=lax.Precision.HIGHEST, preferred_element_type=f32)
+
+
+def small_call(body, out_shape, *args):
+    return pl.pallas_call(body, out_shape=out_shape, compiler_params=pltpu.CompilerParams(vmem_limit_bytes=8 << 20))(*args)
 
 
 def on_device(query_in, key_in, value_in, cotangent, filter_taps):
     length, width = query_in.shape
     local_groups, span = filter_taps.shape
     group_size = width // local_groups
+    across, along = lax.axis_size("ctx"), lax.axis_size("tp")
+    inverse = 1.0 / math.sqrt(length * across * group_size)
+    limit = clip_ratio * math.sqrt(local_groups * along * span)
     after = shifted(cotangent[:span] * query_in[:span], "ctx", -1)
     before = shifted(key_in[length - span :] * value_in[length - span :], "ctx", 1)
-    query_grad, key_grad, value_grad, raw = main_part(query_in, key_in, value_in, cotangent, filter_taps, before, after)
-    inverse = 1.0 / math.sqrt(length * lax.axis_size("ctx") * group_size)
-    limit = clip_ratio * math.sqrt(local_groups * lax.axis_size("tp") * span)
-    scaled = butterfly(raw, "ctx") * inverse
-    squares = butterfly(jnp.broadcast_to(jnp.sum(scaled * scaled), (8, LANES)), "tp")[0, 0]
-    factor = jnp.minimum(1.0, limit / jnp.sqrt(squares + epsilon))
-    return (query_grad, key_grad, value_grad, scaled * factor)
+    query_grad, key_grad, value_grad, inner, first, last, lower = main_part(query_in, key_in, value_in, cotangent, filter_taps)
+    wide = min(width, 1024)
+    raw = edge_raw(key_in, value_in, after, inner, wide)
+    query_grad, = edge_outputs(edge_query_body, False, before, first, lower, [cotangent], [query_grad], wide)
+    key_grad, value_grad = edge_outputs(edge_key_body, True, after, last, lower, [key_in, value_in], [key_grad, value_grad], wide)
+    for masks in rounds(powers(2, across)):
+        received = partners(raw, [(m, 0) for m in masks])
+        if masks[0] == 2:
+            *received, query_grad = lax.optimization_barrier((*received, query_grad))
+        raw = summed(raw, received)
+    masks = [(1, 0), (0, 2), (1, 2)] if along > 2 else [(1, 0)]
+    shapes = (jax.ShapeDtypeStruct(raw.shape, f32), jax.ShapeDtypeStruct((8, LANES), f32))
+    *received, key_grad, value_grad = lax.optimization_barrier((*partners(raw, masks), key_grad, value_grad))
+    scaled, squares = small_call(lambda *refs: norm_body(inverse, *refs), shapes, raw, *received)
+    steps = [1] + powers(4, along)
+    for step in steps[:-1]:
+        squares = squares + partners(squares, [(0, step)])[0]
+    filter_grad = small_call(lambda *refs: scale_body(limit, *refs), shapes[0], scaled, squares, *partners(squares, [(0, steps[-1])]))
+    return (query_grad, key_grad, value_grad, filter_grad)
 
 
 def solution(mesh):

time: 80.4 us -> 65.6 us (0.82)
  waiting for transfers between devices: 29.8 us -> 2.48 us
  Pallas kernels: 25.4 us -> 42.9 us
  other arithmetic: 5.08 us -> 2.53 us
  starting transfers between devices: 16.5 us -> 15.1 us
    ppermute x2, waiting for transfers between devices: 19.8 us -> 0.01 us  [shifted(): lax.ppermute(value, axis, [(source, source + steps) for source in range(f...]
    pallas_call x0 -> x5, Pallas kernels: none -> 15.6 us  [the longest x2 9.4 us: edge_outputs(): pl.pallas_call(body, grid=(width // wide,), in_specs=[head, head, some] +...]
    ppermute x5 -> x7, waiting for transfers between devices: 9.96 us -> 2.48 us  [partners(): lax.ppermute(value, ('ctx', 'tp'), [(i, i ^ c * along + t) for i in numbe...]
    ppermute x5 -> x7, starting transfers between devices: 10.3 us -> 8.32 us  [partners(): lax.ppermute(value, ('ctx', 'tp'), [(i, i ^ c * along + t) for i in numbe...]
    pallas_call x1, Pallas kernels: 25.4 us -> 27.3 us  [main_part(): pl.pallas_call(main_body, grid=(width // WIDE,), in_specs=[block] * 4 + [...]
    add x4 -> x1, other arithmetic: 1.32 us -> 0.02 us  [summed(): return value + received[0] + (received[1] + received[2])]
    unnamed x2 -> x6, local copies, waits for them, and re-layouts: 0.84 us -> 1.63 us
  transfers between devices with their start and end apart: 7 -> 9, of which waited for: 6 -> 2; matrix products, arithmetic and copies ran while one was open for 2% -> 2% of each run, Pallas kernels for 0% -> 64%
where the time goes in v2:
time: 65.6 us; the launch traced here: 65.4 us
  Pallas kernels  42.9 us (65%)
  starting transfers between devices  15.1 us (23%)
  other arithmetic  2.53 us (4%)
  waiting for transfers between devices  2.48 us (4%)
  local copies, waits for them, and re-layouts  1.63 us (2%)
  between operations  0.71 us (1%)
    pallas_call x1, Pallas kernels, main_part(): pl.pallas_call(main_body, grid=(width // WIDE,), in_specs=[block] * 4 + [...  27.3 us
    pallas_call x2, Pallas kernels, edge_outputs(): pl.pallas_call(body, grid=(width // wide,), in_specs=[head, head, some] +...  9.4 us
    ppermute x7, starting transfers between devices, partners(): lax.ppermute(value, ('ctx', 'tp'), [(i, i ^ c * along + t) for i in numbe...  8.32 us
    ppermute x2, starting transfers between devices, shifted(): lax.ppermute(value, axis, [(source, source + steps) for source in range(f...  6.8 us
    pallas_call x1, Pallas kernels, edge_raw(): pl.pallas_call(edge_raw_body, grid=(width // wide,), in_specs=[tail, tail...  5.24 us
    ppermute x7, waiting for transfers between devices, partners(): lax.ppermute(value, ('ctx', 'tp'), [(i, i ^ c * along + t) for i in numbe...  2.48 us
    unnamed x6, local copies, waits for them, and re-layouts  1.63 us
  transfers between devices with their start and end apart: 9, of which 2 were waited for; matrix products, arithmetic and copies ran while one was open for 2% of the time, Pallas kernels for 64%

profile of v2, /device:TPU:0, one launch (start us, length us, event | category | flops | bytes accessed | tf_op | source)
XLA Modules:
  0.0 65.4 jit_solution(5380201447700783010)
XLA Ops:
  0.6 1.3 %slice_multiply_fusion.1 = bf16[128,2048]{1,0:T(8,128)(2,1)S(1)} fusion(bf16[1536,2048]{1,0:T(8,128)(2,1)} %q_ref.1, bf16[1536,2048]{1,0:T(8,128)(2,1)} %c_ref.3), kind=kLoop, calls=%fused_computation.1 | loop fusion | flops 262144 | bytes 1572864 | tf_op jit(solution)/shard_map/mul | solution.py:276
  1.9 1.3 %collective-permute-start = (bf16[128,2048]{1,0:T(8,128)(2,1)S(1)}, bf16[128,2048]{1,0:T(8,128)(2,1)S(1)}, u32[]{:S(2)}, u32[]{:S(2)}) collective-permute-start(bf16[128,2048]{1,0:T(8,128)(2,1)S(1)} %slice_multiply_fusion.1), channel_id=1, source_target_pairs={{4,0},{8,4},{12,8},{16,12},{20,16},{24,20},{28,24},{5,1},{9,5},{13... | collective-permute-start | bytes 1572872 | tf_op jit(solution)/shard_map/ppermute | solution.py:24
  3.2 1.3 %slice_multiply_fusion = bf16[128,2048]{1,0:T(8,128)(2,1)S(1)} fusion(bf16[1536,2048]{1,0:T(8,128)(2,1)} %v_ref.5, bf16[1536,2048]{1,0:T(8,128)(2,1)} %k_ref.5), kind=kLoop, calls=%fused_computation | loop fusion | flops 262144 | bytes 1572864 | tf_op jit(solution)/shard_map/mul | solution.py:277
  4.5 5.5 %collective-permute-start.4 = (bf16[128,2048]{1,0:T(8,128)(2,1)S(1)}, bf16[128,2048]{1,0:T(8,128)(2,1)S(1)}, u32[]{:S(2)}, u32[]{:S(2)}) collective-permute-start(bf16[128,2048]{1,0:T(8,128)(2,1)S(1)} %slice_multiply_fusion), channel_id=1, source_target_pairs={{0,4},{4,8},{8,12},{12,16},{16,20},{20,24},{24,28},{1,5},{5,9},{9,... | collective-permute-start | bytes 1572872 | tf_op jit(solution)/shard_map/ppermute | solution.py:24
  10.0 27.3 %shard_map.84 = (bf16[1536,2048]{1,0:T(8,128)(2,1)}, bf16[1536,2048]{1,0:T(8,128)(2,1)}, bf16[1536,2048]{1,0:T(8,128)(2,1)}, bf16[8,2048,128]{2,1,0:T(8,128)(2,1...) custom-call(bf16[1536,2048]{1,0:T(8,128)(2,1)} %q_ref.1, ...), custom_call_target="tpu_custom_call" | custom-call | flops 4831838208 | bytes 44040192 | tf_op jit(solution)/shard_map/pallas_call | solution.py:141
  37.2 0.0 collective-permute-done.after_ref
  37.2 0.0 copy-start
  37.2 0.8 %copy-done = bf16[128,2048]{1,0:T(8,128)(2,1)} copy-done((bf16[128,2048]{1,0:T(8,128)(2,1)}, bf16[128,2048]{1,0:T(8,128)(2,1)S(1)}, u32[]{:S(2)}) %copy-start) | copy-done | bytes 524312
  38.1 5.2 %shard_map.85 = f32[128,128]{1,0:T(8,128)} custom-call(bf16[1536,2048]{1,0:T(8,128)(2,1)} %k_ref.5, bf16[1536,2048]{1,0:T(8,128)(2,1)} %v_ref.5, bf16[128,2048]{1,0:T(8,128)(2,1)} %copy-done, bf16[8,2048,128]{2,1,0:T(8,128)(2,1)} %get-tuple-element.24.inner_ref), custom_call_target="tpu_custom_call" | custom-call | flops 67108864 | bytes 3670016 | tf_op jit(solution)/shard_map/pallas_call | solution.py:186
  43.3 2.1 %collective-permute-start.1 = (f32[128,128]{1,0:T(8,128)}, f32[128,128]{1,0:T(8,128)S(1)}, u32[]{:S(2)}, u32[]{:S(2)}) collective-permute-start(f32[128,128]{1,0:T(8,128)} %shard_map.85), channel_id=1, source_target_pairs={{0,8},{1,9},{2,10},{3,11},{4,12},{5,13},{6,14},{7,15},{8,0},{9,1},... | collective-permute-start | bytes 196616 | tf_op jit(solution)/shard_map/ppermute | solution.py:30
  45.4 2.6 %collective-permute-start.2 = (f32[128,128]{1,0:T(8,128)}, f32[128,128]{1,0:T(8,128)S(1)}, u32[]{:S(2)}, u32[]{:S(2)}) collective-permute-start(f32[128,128]{1,0:T(8,128)} %shard_map.85), channel_id=1, source_target_pairs={{0,16},{1,17},{2,18},{3,19},{4,20},{5,21},{6,22},{7,23},{8,24},{9,... | collective-permute-start | bytes 196616 | tf_op jit(solution)/shard_map/ppermute | solution.py:30
  48.0 0.0 collective-permute-start.3
  48.0 0.0 collective-permute-done.4.before_ref
  48.0 0.0 copy-start.1
  48.0 0.8 %copy-done.1 = bf16[128,2048]{1,0:T(8,128)(2,1)} copy-done((bf16[128,2048]{1,0:T(8,128)(2,1)}, bf16[128,2048]{1,0:T(8,128)(2,1)S(1)}, u32[]{:S(2)}) %copy-start.1) | copy-done | bytes 524312
  48.8 0.0 copy-start.2
  48.8 4.1 %shard_map.86 = bf16[1536,2048]{1,0:T(8,128)(2,1)} custom-call(bf16[128,2048]{1,0:T(8,128)(2,1)} %copy-done.1, bf16[128,2048]{1,0:T(8,128)(2,1)} %get-tuple-element.25.first_ref, bf16[128,128,128]{2,1,0:T(8,128)(2,1)} %get-tuple-element.26.lower_ref, bf16[1536,2048]{1,0:T(8,128)(2,1)} %c_ref.3, ...), custom_call_target="tpu_custom_call", output_to_operand_aliasing={{}: (4, {})} | custom-call | flops 67108864 | bytes 3145728 | tf_op jit(solution)/shard_map/pallas_call | solution.py:232
  52.9 0.0 collective-permute-done.1
  52.9 0.0 collective-permute-done.2
  53.0 1.3 %collective-permute-done.3 = f32[128,128]{1,0:T(8,128)S(1)} collective-permute-done((f32[128,128]{1,0:T(8,128)}, f32[128,128]{1,0:T(8,128)S(1)}, u32[]{:S(2)}, u32[]{:S(2)}) %collective-permute-start.3) | collective-permute-done | bytes 65568 | tf_op jit(solution)/shard_map/ppermute | solution.py:30
  54.3 0.0 copy-done.2
  54.3 1.4 %collective-permute-start.5 = (f32[128,128]{1,0:T(8,128)S(1)}, f32[128,128]{1,0:T(8,128)S(1)}, u32[]{:S(2)}, u32[]{:S(2)}) collective-permute-start(f32[128,128]{1,0:T(8,128)S(1)} %add_add_fusion.refs_0_), channel_id=1, source_target_pairs={{0,4},{1,5},{2,6},{3,7},{4,0},{5,1},{6,2},{7,3},{8,12},{9,13},{10,... | collective-permute-start | bytes 196616 | tf_op jit(solution)/shard_map/ppermute | solution.py:30
  55.6 1.5 %collective-permute-start.6 = (f32[128,128]{1,0:T(8,128)S(1)}, f32[128,128]{1,0:T(8,128)S(1)}, u32[]{:S(2)}, u32[]{:S(2)}) collective-permute-start(f32[128,128]{1,0:T(8,128)S(1)} %add_add_fusion.refs_0_), channel_id=1, source_target_pairs={{0,2},{1,3},{2,0},{3,1},{4,6},{5,7},{6,4},{7,5},{8,10},{9,11},{10,... | collective-permute-start | bytes 196616 | tf_op jit(solution)/shard_map/ppermute | solution.py:30
  57.2 0.7 %collective-permute-start.7 = (f32[128,128]{1,0:T(8,128)S(1)}, f32[128,128]{1,0:T(8,128)S(1)}, u32[]{:S(2)}, u32[]{:S(2)}) collective-permute-start(f32[128,128]{1,0:T(8,128)S(1)} %add_add_fusion.refs_0_), channel_id=1, source_target_pairs={{0,6},{1,7},{2,4},{3,5},{4,2},{5,3},{6,0},{7,1},{8,14},{9,15},{10,... | collective-permute-start | bytes 196616 | tf_op jit(solution)/shard_map/ppermute | solution.py:30
  57.8 5.3 %shard_map.87 = (bf16[1536,2048]{1,0:T(8,128)(2,1)}, bf16[1536,2048]{1,0:T(8,128)(2,1)}) custom-call(bf16[128,2048]{1,0:T(8,128)(2,1)} %copy-done, bf16[128,2048]{1,0:T(8,128)(2,1)} %get-tuple-element.32.last_ref, bf16[128,128,128]{2,1,0:T(8,128)(2,1)} %get-tuple-element.26.lower_ref, ...), custom_call_target="tpu_custom_call", output_to_operand_aliasing={{0}: (5, {}), {1}: (6, {})} | custom-call | flops 67108864 | bytes 3145728 | tf_op jit(solution)/shard_map/pallas_call | solution.py:232
  63.1 0.0 collective-permute-done.5.refs_1_
  63.1 0.0 collective-permute-done.6.refs_2_
  63.1 0.0 collective-permute-done.7.refs_3_
  63.1 0.1 shard_map.88
  63.3 0.1 collective-permute-start.8
  63.4 1.2 %collective-permute-done.8.refs_2_ = f32[8,128]{1,0:T(8,128)S(1)} collective-permute-done((f32[8,128]{1,0:T(8,128)S(1)}, f32[8,128]{1,0:T(8,128)S(1)}, u32[]{:S(2)}, u32[]{:S(2)}) %collective-permute-start.8) | collective-permute-done | bytes 4128 | tf_op jit(solution)/shard_map/ppermute | solution.py:30
  64.5 0.8 %shard_map.89 = f32[128,128]{1,0:T(8,128)} custom-call(f32[128,128]{1,0:T(8,128)S(1)} %get-tuple-element.42.refs_0_, f32[8,128]{1,0:T(8,128)S(1)} %get-tuple-element.43.refs_1_, f32[8,128]{1,0:T(8,128)S(1)} %collective-permute-done.8.refs_2_), custom_call_target="tpu_custom_call" | custom-call | tf_op jit(solution)/shard_map/pallas_call | solution.py:266
  (1 shorter events, 0.0 us)
Async XLA Ops:
  1.9 35.3 %collective-permute-start = (bf16[128,2048]{1,0:T(8,128)(2,1)S(1)}, bf16[128,2048]{1,0:T(8,128)(2,1)S(1)}, u32[]{:S(2)}, u32[]{:S(2)}) collective-permute-start(bf16[128,2048]{1,0:T(8,128)(2,1)S(1)} %slice_multiply_fusion.1), channel_id=1, source_target_pairs={{4,0},{8,4},{12,8},{16,12},{20,16},{24,20},{28,24},{5,1},{9,5},{13... | collective-permute-start | bytes 1572872 | tf_op jit(solution)/shard_map/ppermute | solution.py:24
  4.5 43.5 %collective-permute-start.4 = (bf16[128,2048]{1,0:T(8,128)(2,1)S(1)}, bf16[128,2048]{1,0:T(8,128)(2,1)S(1)}, u32[]{:S(2)}, u32[]{:S(2)}) collective-permute-start(bf16[128,2048]{1,0:T(8,128)(2,1)S(1)} %slice_multiply_fusion), channel_id=1, source_target_pairs={{0,4},{4,8},{8,12},{12,16},{16,20},{20,24},{24,28},{1,5},{5,9},{9,... | collective-permute-start | bytes 1572872 | tf_op jit(solution)/shard_map/ppermute | solution.py:24
  37.2 0.8 %copy-start = (bf16[128,2048]{1,0:T(8,128)(2,1)}, bf16[128,2048]{1,0:T(8,128)(2,1)S(1)}, u32[]{:S(2)}) copy-start(bf16[128,2048]{1,0:T(8,128)(2,1)S(1)} %collective-permute-done.after_ref) | copy-start | bytes 1572868
  43.3 9.6 %collective-permute-start.1 = (f32[128,128]{1,0:T(8,128)}, f32[128,128]{1,0:T(8,128)S(1)}, u32[]{:S(2)}, u32[]{:S(2)}) collective-permute-start(f32[128,128]{1,0:T(8,128)} %shard_map.85), channel_id=1, source_target_pairs={{0,8},{1,9},{2,10},{3,11},{4,12},{5,13},{6,14},{7,15},{8,0},{9,1},... | collective-permute-start | bytes 196616 | tf_op jit(solution)/shard_map/ppermute | solution.py:30
  45.4 7.6 %collective-permute-start.2 = (f32[128,128]{1,0:T(8,128)}, f32[128,128]{1,0:T(8,128)S(1)}, u32[]{:S(2)}, u32[]{:S(2)}) collective-permute-start(f32[128,128]{1,0:T(8,128)} %shard_map.85), channel_id=1, source_target_pairs={{0,16},{1,17},{2,18},{3,19},{4,20},{5,21},{6,22},{7,23},{8,24},{9,... | collective-permute-start | bytes 196616 | tf_op jit(solution)/shard_map/ppermute | solution.py:30
  48.0 6.3 %collective-permute-start.3 = (f32[128,128]{1,0:T(8,128)}, f32[128,128]{1,0:T(8,128)S(1)}, u32[]{:S(2)}, u32[]{:S(2)}) collective-permute-start(f32[128,128]{1,0:T(8,128)} %shard_map.85), channel_id=1, source_target_pairs={{0,24},{1,25},{2,26},{3,27},{4,28},{5,29},{6,30},{7,31},{8,16},{9,... | collective-permute-start | bytes 196616 | tf_op jit(solution)/shard_map/ppermute | solution.py:30
  48.0 0.8 %copy-start.1 = (bf16[128,2048]{1,0:T(8,128)(2,1)}, bf16[128,2048]{1,0:T(8,128)(2,1)S(1)}, u32[]{:S(2)}) copy-start(bf16[128,2048]{1,0:T(8,128)(2,1)S(1)} %collective-permute-done.4.before_ref) | copy-start | bytes 1572868
  48.8 5.5 %copy-start.2 = (f32[128,128]{1,0:T(8,128)S(1)}, f32[128,128]{1,0:T(8,128)}, u32[]{:S(2)}) copy-start(f32[128,128]{1,0:T(8,128)} %shard_map.85) | copy-start | bytes 196612
  54.3 8.8 %collective-permute-start.5 = (f32[128,128]{1,0:T(8,128)S(1)}, f32[128,128]{1,0:T(8,128)S(1)}, u32[]{:S(2)}, u32[]{:S(2)}) collective-permute-start(f32[128,128]{1,0:T(8,128)S(1)} %add_add_fusion.refs_0_), channel_id=1, source_target_pairs={{0,4},{1,5},{2,6},{3,7},{4,0},{5,1},{6,2},{7,3},{8,12},{9,13},{10,... | collective-permute-start | bytes 196616 | tf_op jit(solution)/shard_map/ppermute | solution.py:30
  55.6 7.5 %collective-permute-start.6 = (f32[128,128]{1,0:T(8,128)S(1)}, f32[128,128]{1,0:T(8,128)S(1)}, u32[]{:S(2)}, u32[]{:S(2)}) collective-permute-start(f32[128,128]{1,0:T(8,128)S(1)} %add_add_fusion.refs_0_), channel_id=1, source_target_pairs={{0,2},{1,3},{2,0},{3,1},{4,6},{5,7},{6,4},{7,5},{8,10},{9,11},{10,... | collective-permute-start | bytes 196616 | tf_op jit(solution)/shard_map/ppermute | solution.py:30
  57.2 6.0 %collective-permute-start.7 = (f32[128,128]{1,0:T(8,128)S(1)}, f32[128,128]{1,0:T(8,128)S(1)}, u32[]{:S(2)}, u32[]{:S(2)}) collective-permute-start(f32[128,128]{1,0:T(8,128)S(1)} %add_add_fusion.refs_0_), channel_id=1, source_target_pairs={{0,6},{1,7},{2,4},{3,5},{4,2},{5,3},{6,0},{7,1},{8,14},{9,15},{10,... | collective-permute-start | bytes 196616 | tf_op jit(solution)/shard_map/ppermute | solution.py:30
  63.3 1.2 %collective-permute-start.8 = (f32[8,128]{1,0:T(8,128)S(1)}, f32[8,128]{1,0:T(8,128)S(1)}, u32[]{:S(2)}, u32[]{:S(2)}) collective-permute-start(f32[8,128]{1,0:T(8,128)S(1)} %get-tuple-element.43.refs_1_), channel_id=1, source_target_pairs={{0,1},{1,0},{2,3},{3,2},{4,5},{5,4},{6,7},{7,6},{8,9},{9,8},{10,11... | collective-permute-start | bytes 12296 | tf_op jit(solution)/shard_map/ppermute | solution.py:30

commit v3 on v2

--- a/solution.py
+++ b/solution.py
@@ -12,6 +12,7 @@
 LANES = 128
 TILE = 16
 WIDE = 256
+CHUNK = 2
 VMEM = 60 << 20
 EDGE_VMEM = 61 << 20
 bf16 = jnp.bfloat16
@@ -67,14 +68,16 @@
     return jnp.concatenate(upper, 0), jnp.concatenate(lower, 0)
 
 
-def diagonal_sums(folded, groups):
-    total = jnp.zeros((groups * TILE, LANES), f32)
+def diagonal_shifts():
     source = lax.broadcasted_iota(jnp.int32, (LANES, LANES), 0)
     target = lax.broadcasted_iota(jnp.int32, (LANES, LANES), 1)
-    for a in range(0, LANES // TILE, 2):
-        left = jnp.concatenate([folded[a], folded[a + 1]], 1)
-        right = [((source + target) % LANES == TILE * (a + i)).astype(bf16) for i in range(2)]
-        total = total + jnp.dot(left, jnp.concatenate(right, 0), preferred_element_type=f32)
+    return jnp.concatenate([((source + target) % LANES == a).astype(bf16) for a in range(0, LANES, TILE)], 0)
+
+
+def diagonal_sums(folded, shifts, first, groups):
+    at = slice(first * TILE, (first + groups) * TILE)
+    left = jnp.concatenate([folded[a, at, :] for a in range(LANES // TILE)], 1)
+    total = jnp.dot(left, shifts, preferred_element_type=f32)
     sums = []
     for g in range(groups):
         part = pltpu.roll(total[g * TILE : (g + 1) * TILE], 0, 1, stride=1, stride_axis=0)
@@ -90,42 +93,61 @@
     lane = lax.broadcasted_iota(jnp.int32, (TILE, LANES), 1)
     row = lax.broadcasted_iota(jnp.int32, (TILE, LANES), 0)
     flat = lambda x: x.reshape(blocks * group, LANES)
-    for h in range(width // LANES):
-        cols = slice(h * LANES, (h + 1) * LANES)
+    per = LANES // group
+    halves = width // LANES
+
+    def enter(h, b):
+        cols, rows = slice(h * LANES, (h + 1) * LANES), slice(b * LANES, (b + 1) * LANES)
+        mixed = k_ref[rows, cols] * v_ref[rows, cols]
+        mt[h, b + 1] = mixed.T
+        st[h, b] = (c_ref[rows, cols] * q_ref[rows, cols]).T
+
+    def convolve(h, p):
+        g = h * per + p
+        own = slice(p * group, (p + 1) * group)
+        upper, lower = toeplitz(taps_ref[g : g + 1, :])
+        lower_ref[g] = lower
+        mixed = flat(mt[h, 1 : blocks + 1, own, :])
+        window = jnp.concatenate([flat(mt[h, :blocks, own, :]), mixed], 1)
+        ahead = jnp.concatenate([flat(st[h, :blocks, own, :]), flat(st[h, 1 : blocks + 1, own, :])], 1)
+        conv = jnp.dot(window, jnp.concatenate([lower, upper], 0), preferred_element_type=f32)
+        back = lax.dot_general(ahead, jnp.concatenate([upper, lower], 1), (((1,), (1,)), ((), ())), preferred_element_type=f32)
+        ct[h, :, own, :] = conv.astype(bf16).reshape(blocks, group, LANES)
+        bt[h, :, own, :] = back.astype(bf16).reshape(blocks, group, LANES)
+        gram = lax.dot_general(mixed, ahead, (((0,), (0,)), ((), ())), preferred_element_type=f32)
+        for a in range(LANES // TILE):
+            rows = slice(a * TILE, (a + 1) * TILE)
+            kept = jnp.where(lane >= row + a * TILE, gram[rows, :LANES], gram[rows, LANES:])
+            folded[a, g * TILE : (g + 1) * TILE, :] = kept.astype(bf16)
+
+    def leave(h, b):
+        cols, rows = slice(h * LANES, (h + 1) * LANES), slice(b * LANES, (b + 1) * LANES)
+        conv = ct[h, b].T
+        back = bt[h, b].T
+        if b == 0:
+            first_ref[:, cols] = conv
+        if b == blocks - 1:
+            last_ref[:, cols] = back
+        dq_ref[rows, cols] = c_ref[rows, cols] * conv
+        dk_ref[rows, cols] = v_ref[rows, cols] * back
+        dv_ref[rows, cols] = k_ref[rows, cols] * back
+
+    share = 3
+    for h in range(halves):
         mt[h, 0] = jnp.zeros((LANES, LANES), bf16)
         st[h, blocks] = jnp.zeros((LANES, LANES), bf16)
-        for b in range(blocks):
-            rows = slice(b * LANES, (b + 1) * LANES)
-            mt[h, b + 1] = (k_ref[rows, cols] * v_ref[rows, cols]).T
-            st[h, b] = (c_ref[rows, cols] * q_ref[rows, cols]).T
-        for p in range(LANES // group):
-            g = h * (LANES // group) + p
-            own = slice(p * group, (p + 1) * group)
-            upper, lower = toeplitz(taps_ref[g : g + 1, :])
-            lower_ref[g] = lower
-            mixed = flat(mt[h, 1 : blocks + 1, own, :])
-            window = jnp.concatenate([flat(mt[h, :blocks, own, :]), mixed], 1)
-            ahead = jnp.concatenate([flat(st[h, :blocks, own, :]), flat(st[h, 1 : blocks + 1, own, :])], 1)
-            conv = jnp.dot(window, jnp.concatenate([lower, upper], 0), preferred_element_type=f32)
-            back = lax.dot_general(ahead, jnp.concatenate([upper, lower], 1), (((1,), (1,)), ((), ())), preferred_element_type=f32)
-            ct[h, :, own, :] = conv.astype(bf16).reshape(blocks, group, LANES)
-            bt[h, :, own, :] = back.astype(bf16).reshape(blocks, group, LANES)
-            gram = lax.dot_general(mixed, ahead, (((0,), (0,)), ((), ())), preferred_element_type=f32)
-            for a in range(LANES // TILE):
-                rows = slice(a * TILE, (a + 1) * TILE)
-                kept = jnp.where(lane >= row + a * TILE, gram[rows, :LANES], gram[rows, LANES:])
-                folded[a, g * TILE : (g + 1) * TILE, :] = kept.astype(bf16)
-        for b in range(blocks):
-            rows = slice(b * LANES, (b + 1) * LANES)
-            conv = ct[h, b].T
-            back = bt[h, b].T
-            if b == 0:
-                first_ref[:, cols] = conv
-            if b == blocks - 1:
-                last_ref[:, cols] = back
-            dq_ref[rows, cols] = c_ref[rows, cols] * conv
-            dk_ref[rows, cols] = v_ref[rows, cols] * back
-            dv_ref[rows, cols] = k_ref[rows, cols] * back
+    for b in range(blocks):
+        enter(0, b)
+    for h in range(halves):
+        for p in range(per):
+            convolve(h, p)
+            for b in range(p * share, min(blocks, (p + 1) * share)):
+                if h + 1 < halves:
+                    enter(h + 1, b)
+                if h > 0:
+                    leave(h - 1, b)
+    for b in range(blocks):
+        leave(halves - 1, b)
 
 
 def main_part(q, k, v, c, taps):
@@ -159,6 +181,12 @@
     row = lax.broadcasted_iota(jnp.int32, (TILE, LANES), 0)
     per = LANES // group
     zero = jnp.zeros((TILE, LANES), bf16)
+    shifts = diagonal_shifts()
+    chunk = CHUNK * per
+
+    def finish(first):
+        out_ref[first : first + chunk, :] = diagonal_sums(folded, shifts, first, chunk)
+
     for h in range(width // LANES):
         cols = slice(h * LANES, (h + 1) * LANES)
         mixed = k_ref[:, cols] * v_ref[:, cols]
@@ -173,7 +201,9 @@
                 for a in range(LANES // TILE):
                     part = gram[a * TILE : (a + 1) * TILE, n * LANES : (n + 1) * LANES].astype(bf16)
                     folded[a, at, :] = inner_ref[a, at, :] + jnp.where(lane < row + a * TILE, part, zero)
-    out_ref[...] = diagonal_sums(folded, groups)
+        if h % CHUNK == 0 and h >= CHUNK:
+            finish((h - CHUNK) * per)
+    finish(groups - chunk)
 
 
 def edge_raw(k, v, after, inner, wide):

time: 65.6 us -> 63.1 us (0.962)
  Pallas kernels: 42.9 us -> 40.5 us
    pallas_call x1, Pallas kernels: 27.3 us -> 24.6 us  [main_part(): pl.pallas_call(main_body, grid=(width // WIDE,), in_specs=[block] * 4 + [...]
  transfers between devices with their start and end apart: 9 -> 9, of which waited for: 2 -> 2; matrix products, arithmetic and copies ran while one was open for 2% -> 2% of each run, Pallas kernels for 64% -> 63%
where the time goes in v3:
time: 63.1 us; the launch traced here: 62.9 us
  Pallas kernels  40.5 us (64%)
  starting transfers between devices  15.1 us (24%)
  other arithmetic  2.53 us (4%)
  waiting for transfers between devices  2.48 us (4%)
  local copies, waits for them, and re-layouts  1.63 us (3%)
  between operations  0.71 us (1%)
    pallas_call x1, Pallas kernels, main_part(): pl.pallas_call(main_body, grid=(width // WIDE,), in_specs=[block] * 4 + [...  24.6 us
    pallas_call x2, Pallas kernels, edge_outputs(): pl.pallas_call(body, grid=(width // wide,), in_specs=[head, head, some] +...  9.4 us
    ppermute x7, starting transfers between devices, partners(): lax.ppermute(value, ('ctx', 'tp'), [(i, i ^ c * along + t) for i in numbe...  8.31 us
    ppermute x2, starting transfers between devices, shifted(): lax.ppermute(value, axis, [(source, source + steps) for source in range(f...  6.8 us
    pallas_call x1, Pallas kernels, edge_raw(): pl.pallas_call(edge_raw_body, grid=(width // wide,), in_specs=[tail, tail...  5.5 us
    ppermute x7, waiting for transfers between devices, partners(): lax.ppermute(value, ('ctx', 'tp'), [(i, i ^ c * along + t) for i in numbe...  2.48 us
    unnamed x6, local copies, waits for them, and re-layouts  1.63 us
  transfers between devices with their start and end apart: 9, of which 2 were waited for; matrix products, arithmetic and copies ran while one was open for 2% of the time, Pallas kernels for 63%

profile of v3, /device:TPU:0, one launch (start us, length us, event | category | flops | bytes accessed | tf_op | source)
XLA Modules:
  0.0 62.9 jit_solution(13526946013235734538)
XLA Ops:
  0.6 1.3 %slice_multiply_fusion.1 = bf16[128,2048]{1,0:T(8,128)(2,1)S(1)} fusion(bf16[1536,2048]{1,0:T(8,128)(2,1)} %q_ref.1, bf16[1536,2048]{1,0:T(8,128)(2,1)} %c_ref.3), kind=kLoop, calls=%fused_computation.1 | loop fusion | flops 262144 | bytes 1572864 | tf_op jit(solution)/shard_map/mul | solution.py:306
  1.9 1.3 %collective-permute-start = (bf16[128,2048]{1,0:T(8,128)(2,1)S(1)}, bf16[128,2048]{1,0:T(8,128)(2,1)S(1)}, u32[]{:S(2)}, u32[]{:S(2)}) collective-permute-start(bf16[128,2048]{1,0:T(8,128)(2,1)S(1)} %slice_multiply_fusion.1), channel_id=1, source_target_pairs={{4,0},{8,4},{12,8},{16,12},{20,16},{24,20},{28,24},{5,1},{9,5},{13... | collective-permute-start | bytes 1572872 | tf_op jit(solution)/shard_map/ppermute | solution.py:25
  3.2 1.3 %slice_multiply_fusion = bf16[128,2048]{1,0:T(8,128)(2,1)S(1)} fusion(bf16[1536,2048]{1,0:T(8,128)(2,1)} %v_ref.5, bf16[1536,2048]{1,0:T(8,128)(2,1)} %k_ref.5), kind=kLoop, calls=%fused_computation | loop fusion | flops 262144 | bytes 1572864 | tf_op jit(solution)/shard_map/mul | solution.py:307
  4.5 5.5 %collective-permute-start.4 = (bf16[128,2048]{1,0:T(8,128)(2,1)S(1)}, bf16[128,2048]{1,0:T(8,128)(2,1)S(1)}, u32[]{:S(2)}, u32[]{:S(2)}) collective-permute-start(bf16[128,2048]{1,0:T(8,128)(2,1)S(1)} %slice_multiply_fusion), channel_id=1, source_target_pairs={{0,4},{4,8},{8,12},{12,16},{16,20},{20,24},{24,28},{1,5},{5,9},{9,... | collective-permute-start | bytes 1572872 | tf_op jit(solution)/shard_map/ppermute | solution.py:25
  10.0 24.6 %shard_map.84 = (bf16[1536,2048]{1,0:T(8,128)(2,1)}, bf16[1536,2048]{1,0:T(8,128)(2,1)}, bf16[1536,2048]{1,0:T(8,128)(2,1)}, bf16[8,2048,128]{2,1,0:T(8,128)(2,1...) custom-call(bf16[1536,2048]{1,0:T(8,128)(2,1)} %q_ref.1, ...), custom_call_target="tpu_custom_call" | custom-call | flops 4831838208 | bytes 44040192 | tf_op jit(solution)/shard_map/pallas_call | solution.py:163
  34.5 0.0 collective-permute-done.after_ref
  34.6 0.0 copy-start
  34.6 0.8 %copy-done = bf16[128,2048]{1,0:T(8,128)(2,1)} copy-done((bf16[128,2048]{1,0:T(8,128)(2,1)}, bf16[128,2048]{1,0:T(8,128)(2,1)S(1)}, u32[]{:S(2)}) %copy-start) | copy-done | bytes 524312
  35.4 5.5 %shard_map.85 = f32[128,128]{1,0:T(8,128)} custom-call(bf16[1536,2048]{1,0:T(8,128)(2,1)} %k_ref.5, bf16[1536,2048]{1,0:T(8,128)(2,1)} %v_ref.5, bf16[128,2048]{1,0:T(8,128)(2,1)} %copy-done, bf16[8,2048,128]{2,1,0:T(8,128)(2,1)} %get-tuple-element.24.inner_ref), custom_call_target="tpu_custom_call" | custom-call | flops 67108864 | bytes 3670016 | tf_op jit(solution)/shard_map/pallas_call | solution.py:216
  40.9 2.1 %collective-permute-start.1 = (f32[128,128]{1,0:T(8,128)}, f32[128,128]{1,0:T(8,128)S(1)}, u32[]{:S(2)}, u32[]{:S(2)}) collective-permute-start(f32[128,128]{1,0:T(8,128)} %shard_map.85), channel_id=1, source_target_pairs={{0,8},{1,9},{2,10},{3,11},{4,12},{5,13},{6,14},{7,15},{8,0},{9,1},... | collective-permute-start | bytes 196616 | tf_op jit(solution)/shard_map/ppermute | solution.py:31
  42.9 2.6 %collective-permute-start.2 = (f32[128,128]{1,0:T(8,128)}, f32[128,128]{1,0:T(8,128)S(1)}, u32[]{:S(2)}, u32[]{:S(2)}) collective-permute-start(f32[128,128]{1,0:T(8,128)} %shard_map.85), channel_id=1, source_target_pairs={{0,16},{1,17},{2,18},{3,19},{4,20},{5,21},{6,22},{7,23},{8,24},{9,... | collective-permute-start | bytes 196616 | tf_op jit(solution)/shard_map/ppermute | solution.py:31
  45.6 0.0 collective-permute-start.3
  45.6 0.0 collective-permute-done.4.before_ref
  45.6 0.0 copy-start.1
  45.6 0.8 %copy-done.1 = bf16[128,2048]{1,0:T(8,128)(2,1)} copy-done((bf16[128,2048]{1,0:T(8,128)(2,1)}, bf16[128,2048]{1,0:T(8,128)(2,1)S(1)}, u32[]{:S(2)}) %copy-start.1) | copy-done | bytes 524312
  46.4 0.0 copy-start.2
  46.4 4.1 %shard_map.86 = bf16[1536,2048]{1,0:T(8,128)(2,1)} custom-call(bf16[128,2048]{1,0:T(8,128)(2,1)} %copy-done.1, bf16[128,2048]{1,0:T(8,128)(2,1)} %get-tuple-element.25.first_ref, bf16[128,128,128]{2,1,0:T(8,128)(2,1)} %get-tuple-element.26.lower_ref, bf16[1536,2048]{1,0:T(8,128)(2,1)} %c_ref.3, ...), custom_call_target="tpu_custom_call", output_to_operand_aliasing={{}: (4, {})} | custom-call | flops 67108864 | bytes 3145728 | tf_op jit(solution)/shard_map/pallas_call | solution.py:262
  50.5 0.0 collective-permute-done.1
  50.5 0.0 collective-permute-done.2
  50.5 1.3 %collective-permute-done.3 = f32[128,128]{1,0:T(8,128)S(1)} collective-permute-done((f32[128,128]{1,0:T(8,128)}, f32[128,128]{1,0:T(8,128)S(1)}, u32[]{:S(2)}, u32[]{:S(2)}) %collective-permute-start.3) | collective-permute-done | bytes 65568 | tf_op jit(solution)/shard_map/ppermute | solution.py:31
  51.8 0.0 copy-done.2
  51.9 1.4 %collective-permute-start.5 = (f32[128,128]{1,0:T(8,128)S(1)}, f32[128,128]{1,0:T(8,128)S(1)}, u32[]{:S(2)}, u32[]{:S(2)}) collective-permute-start(f32[128,128]{1,0:T(8,128)S(1)} %add_add_fusion.refs_0_), channel_id=1, source_target_pairs={{0,4},{1,5},{2,6},{3,7},{4,0},{5,1},{6,2},{7,3},{8,12},{9,13},{10,... | collective-permute-start | bytes 196616 | tf_op jit(solution)/shard_map/ppermute | solution.py:31
  53.2 1.5 %collective-permute-start.6 = (f32[128,128]{1,0:T(8,128)S(1)}, f32[128,128]{1,0:T(8,128)S(1)}, u32[]{:S(2)}, u32[]{:S(2)}) collective-permute-start(f32[128,128]{1,0:T(8,128)S(1)} %add_add_fusion.refs_0_), channel_id=1, source_target_pairs={{0,2},{1,3},{2,0},{3,1},{4,6},{5,7},{6,4},{7,5},{8,10},{9,11},{10,... | collective-permute-start | bytes 196616 | tf_op jit(solution)/shard_map/ppermute | solution.py:31
  54.7 0.7 %collective-permute-start.7 = (f32[128,128]{1,0:T(8,128)S(1)}, f32[128,128]{1,0:T(8,128)S(1)}, u32[]{:S(2)}, u32[]{:S(2)}) collective-permute-start(f32[128,128]{1,0:T(8,128)S(1)} %add_add_fusion.refs_0_), channel_id=1, source_target_pairs={{0,6},{1,7},{2,4},{3,5},{4,2},{5,3},{6,0},{7,1},{8,14},{9,15},{10,... | collective-permute-start | bytes 196616 | tf_op jit(solution)/shard_map/ppermute | solution.py:31
  55.4 5.3 %shard_map.87 = (bf16[1536,2048]{1,0:T(8,128)(2,1)}, bf16[1536,2048]{1,0:T(8,128)(2,1)}) custom-call(bf16[128,2048]{1,0:T(8,128)(2,1)} %copy-done, bf16[128,2048]{1,0:T(8,128)(2,1)} %get-tuple-element.32.last_ref, bf16[128,128,128]{2,1,0:T(8,128)(2,1)} %get-tuple-element.26.lower_ref, ...), custom_call_target="tpu_custom_call", output_to_operand_aliasing={{0}: (5, {}), {1}: (6, {})} | custom-call | flops 67108864 | bytes 3145728 | tf_op jit(solution)/shard_map/pallas_call | solution.py:262
  60.7 0.0 collective-permute-done.5.refs_1_
  60.7 0.0 collective-permute-done.6.refs_2_
  60.7 0.0 collective-permute-done.7.refs_3_
  60.7 0.1 shard_map.88
  60.9 0.1 collective-permute-start.8
  60.9 1.2 %collective-permute-done.8.refs_2_ = f32[8,128]{1,0:T(8,128)S(1)} collective-permute-done((f32[8,128]{1,0:T(8,128)S(1)}, f32[8,128]{1,0:T(8,128)S(1)}, u32[]{:S(2)}, u32[]{:S(2)}) %collective-permute-start.8) | collective-permute-done | bytes 4128 | tf_op jit(solution)/shard_map/ppermute | solution.py:31
  62.1 0.8 %shard_map.89 = f32[128,128]{1,0:T(8,128)} custom-call(f32[128,128]{1,0:T(8,128)S(1)} %get-tuple-element.42.refs_0_, f32[8,128]{1,0:T(8,128)S(1)} %get-tuple-element.43.refs_1_, f32[8,128]{1,0:T(8,128)S(1)} %collective-permute-done.8.refs_2_), custom_call_target="tpu_custom_call" | custom-call | tf_op jit(solution)/shard_map/pallas_call | solution.py:296
  (1 shorter events, 0.0 us)
Async XLA Ops:
  1.9 32.7 %collective-permute-start = (bf16[128,2048]{1,0:T(8,128)(2,1)S(1)}, bf16[128,2048]{1,0:T(8,128)(2,1)S(1)}, u32[]{:S(2)}, u32[]{:S(2)}) collective-permute-start(bf16[128,2048]{1,0:T(8,128)(2,1)S(1)} %slice_multiply_fusion.1), channel_id=1, source_target_pairs={{4,0},{8,4},{12,8},{16,12},{20,16},{24,20},{28,24},{5,1},{9,5},{13... | collective-permute-start | bytes 1572872 | tf_op jit(solution)/shard_map/ppermute | solution.py:25
  4.5 41.1 %collective-permute-start.4 = (bf16[128,2048]{1,0:T(8,128)(2,1)S(1)}, bf16[128,2048]{1,0:T(8,128)(2,1)S(1)}, u32[]{:S(2)}, u32[]{:S(2)}) collective-permute-start(bf16[128,2048]{1,0:T(8,128)(2,1)S(1)} %slice_multiply_fusion), channel_id=1, source_target_pairs={{0,4},{4,8},{8,12},{12,16},{16,20},{20,24},{24,28},{1,5},{5,9},{9,... | collective-permute-start | bytes 1572872 | tf_op jit(solution)/shard_map/ppermute | solution.py:25
  34.6 0.8 %copy-start = (bf16[128,2048]{1,0:T(8,128)(2,1)}, bf16[128,2048]{1,0:T(8,128)(2,1)S(1)}, u32[]{:S(2)}) copy-start(bf16[128,2048]{1,0:T(8,128)(2,1)S(1)} %collective-permute-done.after_ref) | copy-start | bytes 1572868
  40.9 9.6 %collective-permute-start.1 = (f32[128,128]{1,0:T(8,128)}, f32[128,128]{1,0:T(8,128)S(1)}, u32[]{:S(2)}, u32[]{:S(2)}) collective-permute-start(f32[128,128]{1,0:T(8,128)} %shard_map.85), channel_id=1, source_target_pairs={{0,8},{1,9},{2,10},{3,11},{4,12},{5,13},{6,14},{7,15},{8,0},{9,1},... | collective-permute-start | bytes 196616 | tf_op jit(solution)/shard_map/ppermute | solution.py:31
  42.9 7.6 %collective-permute-start.2 = (f32[128,128]{1,0:T(8,128)}, f32[128,128]{1,0:T(8,128)S(1)}, u32[]{:S(2)}, u32[]{:S(2)}) collective-permute-start(f32[128,128]{1,0:T(8,128)} %shard_map.85), channel_id=1, source_target_pairs={{0,16},{1,17},{2,18},{3,19},{4,20},{5,21},{6,22},{7,23},{8,24},{9,... | collective-permute-start | bytes 196616 | tf_op jit(solution)/shard_map/ppermute | solution.py:31
  45.6 6.3 %collective-permute-start.3 = (f32[128,128]{1,0:T(8,128)}, f32[128,128]{1,0:T(8,128)S(1)}, u32[]{:S(2)}, u32[]{:S(2)}) collective-permute-start(f32[128,128]{1,0:T(8,128)} %shard_map.85), channel_id=1, source_target_pairs={{0,24},{1,25},{2,26},{3,27},{4,28},{5,29},{6,30},{7,31},{8,16},{9,... | collective-permute-start | bytes 196616 | tf_op jit(solution)/shard_map/ppermute | solution.py:31
  45.6 0.8 %copy-start.1 = (bf16[128,2048]{1,0:T(8,128)(2,1)}, bf16[128,2048]{1,0:T(8,128)(2,1)S(1)}, u32[]{:S(2)}) copy-start(bf16[128,2048]{1,0:T(8,128)(2,1)S(1)} %collective-permute-done.4.before_ref) | copy-start | bytes 1572868
  46.4 5.5 %copy-start.2 = (f32[128,128]{1,0:T(8,128)S(1)}, f32[128,128]{1,0:T(8,128)}, u32[]{:S(2)}) copy-start(f32[128,128]{1,0:T(8,128)} %shard_map.85) | copy-start | bytes 196612
  51.9 8.8 %collective-permute-start.5 = (f32[128,128]{1,0:T(8,128)S(1)}, f32[128,128]{1,0:T(8,128)S(1)}, u32[]{:S(2)}, u32[]{:S(2)}) collective-permute-start(f32[128,128]{1,0:T(8,128)S(1)} %add_add_fusion.refs_0_), channel_id=1, source_target_pairs={{0,4},{1,5},{2,6},{3,7},{4,0},{5,1},{6,2},{7,3},{8,12},{9,13},{10,... | collective-permute-start | bytes 196616 | tf_op jit(solution)/shard_map/ppermute | solution.py:31
  53.2 7.5 %collective-permute-start.6 = (f32[128,128]{1,0:T(8,128)S(1)}, f32[128,128]{1,0:T(8,128)S(1)}, u32[]{:S(2)}, u32[]{:S(2)}) collective-permute-start(f32[128,128]{1,0:T(8,128)S(1)} %add_add_fusion.refs_0_), channel_id=1, source_target_pairs={{0,2},{1,3},{2,0},{3,1},{4,6},{5,7},{6,4},{7,5},{8,10},{9,11},{10,... | collective-permute-start | bytes 196616 | tf_op jit(solution)/shard_map/ppermute | solution.py:31
  54.7 6.0 %collective-permute-start.7 = (f32[128,128]{1,0:T(8,128)S(1)}, f32[128,128]{1,0:T(8,128)S(1)}, u32[]{:S(2)}, u32[]{:S(2)}) collective-permute-start(f32[128,128]{1,0:T(8,128)S(1)} %add_add_fusion.refs_0_), channel_id=1, source_target_pairs={{0,6},{1,7},{2,4},{3,5},{4,2},{5,3},{6,0},{7,1},{8,14},{9,15},{10,... | collective-permute-start | bytes 196616 | tf_op jit(solution)/shard_map/ppermute | solution.py:31
  60.9 1.2 %collective-permute-start.8 = (f32[8,128]{1,0:T(8,128)S(1)}, f32[8,128]{1,0:T(8,128)S(1)}, u32[]{:S(2)}, u32[]{:S(2)}) collective-permute-start(f32[8,128]{1,0:T(8,128)S(1)} %get-tuple-element.43.refs_1_), channel_id=1, source_target_pairs={{0,1},{1,0},{2,3},{3,2},{4,5},{5,4},{6,7},{7,6},{8,9},{9,8},{10,11... | collective-permute-start | bytes 12296 | tf_op jit(solution)/shard_map/ppermute | solution.py:31

commit v4 on v3

--- a/solution.py
+++ b/solution.py
@@ -13,7 +13,7 @@
 TILE = 16
 WIDE = 256
 CHUNK = 2
-VMEM = 60 << 20
+VMEM = 127 << 19
 EDGE_VMEM = 61 << 20
 bf16 = jnp.bfloat16
 f32 = jnp.float32
@@ -303,8 +303,9 @@
     across, along = lax.axis_size("ctx"), lax.axis_size("tp")
     inverse = 1.0 / math.sqrt(length * across * group_size)
     limit = clip_ratio * math.sqrt(local_groups * along * span)
-    after = shifted(cotangent[:span] * query_in[:span], "ctx", -1)
-    before = shifted(key_in[length - span :] * value_in[length - span :], "ctx", 1)
+    signal, mixed = lax.optimization_barrier((cotangent[:span] * query_in[:span], key_in[length - span :] * value_in[length - span :]))
+    after = shifted(signal, "ctx", -1)
+    before = shifted(mixed, "ctx", 1)
     query_grad, key_grad, value_grad, inner, first, last, lower = main_part(query_in, key_in, value_in, cotangent, filter_taps)
     wide = min(width, 1024)
     raw = edge_raw(key_in, value_in, after, inner, wide)
@@ -313,11 +314,11 @@
     for masks in rounds(powers(2, across)):
         received = partners(raw, [(m, 0) for m in masks])
         if masks[0] == 2:
-            *received, query_grad = lax.optimization_barrier((*received, query_grad))
+            *received, key_grad, value_grad = lax.optimization_barrier((*received, key_grad, value_grad))
         raw = summed(raw, received)
     masks = [(1, 0), (0, 2), (1, 2)] if along > 2 else [(1, 0)]
     shapes = (jax.ShapeDtypeStruct(raw.shape, f32), jax.ShapeDtypeStruct((8, LANES), f32))
-    *received, key_grad, value_grad = lax.optimization_barrier((*partners(raw, masks), key_grad, value_grad))
+    *received, query_grad = lax.optimization_barrier((*partners(raw, masks), query_grad))
     scaled, squares = small_call(lambda *refs: norm_body(inverse, *refs), shapes, raw, *received)
     steps = [1] + powers(4, along)
     for step in steps[:-1]:

time: 63.1 us -> 61.1 us (0.968)
  local copies, waits for them, and re-layouts: 1.63 us -> 0.01 us
  waiting for transfers between devices: 2.48 us -> 1.17 us
  starting transfers between devices: 15.1 us -> 15.9 us
    unnamed x6 -> x2, local copies, waits for them, and re-layouts: 1.63 us -> 0.01 us
    mul x1, other arithmetic: 1.26 us -> 2.63 us  [on_device(): key_in[length - span:] * value_in[length - span:]]
    ppermute x7, waiting for transfers between devices: 2.48 us -> 1.17 us  [partners(): lax.ppermute(value, ('ctx', 'tp'), [(i, i ^ c * along + t) for i in numbe...]
    mul x1 -> x0, other arithmetic: 1.26 us -> none  [on_device(): after = shifted(cotangent[:span] * query_in[:span], 'ctx', -1)]
    ppermute x2, starting transfers between devices: 6.8 us -> 7.59 us  [shifted(): lax.ppermute(value, axis, [(source, source + steps) for source in range(f...]
  transfers between devices with their start and end apart: 9 -> 9, of which waited for: 2 -> 1; matrix products, arithmetic and copies ran while one was open for 2% -> 0% of each run, Pallas kernels for 63% -> 65%
where the time goes in v4:
time: 61.1 us; the launch traced here: 60.9 us
  Pallas kernels  40.5 us (66%)
  starting transfers between devices  15.9 us (26%)
  other arithmetic  2.65 us (4%)
  waiting for transfers between devices  1.17 us (2%)
  between operations  0.7 us (1%)
    pallas_call x1, Pallas kernels, main_part(): pl.pallas_call(main_body, grid=(width // WIDE,), in_specs=[block] * 4 + [...  24.6 us
    pallas_call x2, Pallas kernels, edge_outputs(): pl.pallas_call(body, grid=(width // wide,), in_specs=[head, head, some] +...  9.41 us
    ppermute x7, starting transfers between devices, partners(): lax.ppermute(value, ('ctx', 'tp'), [(i, i ^ c * along + t) for i in numbe...  8.31 us
    ppermute x2, starting transfers between devices, shifted(): lax.ppermute(value, axis, [(source, source + steps) for source in range(f...  7.59 us
    pallas_call x1, Pallas kernels, edge_raw(): pl.pallas_call(edge_raw_body, grid=(width // wide,), in_specs=[tail, tail...  5.51 us
    mul x1, other arithmetic, on_device(): key_in[length - span:] * value_in[length - span:]  2.63 us
  transfers between devices with their start and end apart: 9, of which 1 were waited for; matrix products, arithmetic and copies ran while one was open for 0% of the time, Pallas kernels for 65%

profile of v4, /device:TPU:0, one launch (start us, length us, event | category | flops | bytes accessed | tf_op | source)
XLA Modules:
  0.0 60.9 jit_solution(14545512150059610107)
XLA Ops:
  0.6 2.6 %slice_multiply_fusion = (bf16[128,2048]{1,0:T(8,128)(2,1)}, bf16[128,2048]{1,0:T(8,128)(2,1)}) fusion(bf16[1536,2048]{1,0:T(8,128)(2,1)} %v_ref.5, bf16[1536,2048]{1,0:T(8,128)(2,1)} %k_ref.5, bf16[1536,2048]{1,0:T(8,128)(2,1)} %q_ref.1, bf16[1536,2048]{1,0:T(8,128)(2,1)} %c_ref.3), kind=kLoop, calls=%fused_computation | loop fusion | flops 524288 | bytes 3145728 | tf_op jit(solution)/shard_map/mul | solution.py:306
  3.3 1.3 %collective-permute-start = (bf16[128,2048]{1,0:T(8,128)(2,1)}, bf16[128,2048]{1,0:T(8,128)(2,1)}, u32[]{:S(2)}, u32[]{:S(2)}) collective-permute-start(bf16[128,2048]{1,0:T(8,128)(2,1)} %get-tuple-element.26), channel_id=1, source_target_pairs={{4,0},{8,4},{12,8},{16,12},{20,16},{24,20},{28,24},{5,1},{9,5},{13... | collective-permute-start | bytes 1572872 | tf_op jit(solution)/shard_map/ppermute | solution.py:25
  4.5 6.3 %collective-permute-start.7 = (bf16[128,2048]{1,0:T(8,128)(2,1)}, bf16[128,2048]{1,0:T(8,128)(2,1)}, u32[]{:S(2)}, u32[]{:S(2)}) collective-permute-start(bf16[128,2048]{1,0:T(8,128)(2,1)} %get-tuple-element.37), channel_id=1, source_target_pairs={{0,4},{4,8},{8,12},{12,16},{16,20},{20,24},{24,28},{1,5},{5,9},{9,... | collective-permute-start | bytes 1572872 | tf_op jit(solution)/shard_map/ppermute | solution.py:25
  10.9 24.6 %shard_map.84 = (bf16[1536,2048]{1,0:T(8,128)(2,1)}, bf16[1536,2048]{1,0:T(8,128)(2,1)}, bf16[1536,2048]{1,0:T(8,128)(2,1)}, bf16[8,2048,128]{2,1,0:T(8,128)(2,1...) custom-call(bf16[1536,2048]{1,0:T(8,128)(2,1)} %q_ref.1, ...), custom_call_target="tpu_custom_call" | custom-call | flops 4831838208 | bytes 44040192 | tf_op jit(solution)/shard_map/pallas_call | solution.py:163
  35.4 0.0 collective-permute-done.after_ref
  35.4 5.5 %shard_map.85 = f32[128,128]{1,0:T(8,128)} custom-call(bf16[1536,2048]{1,0:T(8,128)(2,1)} %k_ref.5, bf16[1536,2048]{1,0:T(8,128)(2,1)} %v_ref.5, bf16[128,2048]{1,0:T(8,128)(2,1)} %collective-permute-done.after_ref, bf16[8,2048,128]{2,1,0:T(8,128)(2,1)} %get-tuple-element.27.inner_ref), custom_call_target="tpu_custom_call" | custom-call | flops 67108864 | bytes 3670016 | tf_op jit(solution)/shard_map/pallas_call | solution.py:216
  40.9 4.1 %collective-permute-start.3 = (f32[128,128]{1,0:T(8,128)}, f32[128,128]{1,0:T(8,128)S(1)}, u32[]{:S(2)}, u32[]{:S(2)}) collective-permute-start(f32[128,128]{1,0:T(8,128)} %shard_map.85), channel_id=1, source_target_pairs={{0,24},{1,25},{2,26},{3,27},{4,28},{5,29},{6,30},{7,31},{8,16},{9,... | collective-permute-start | bytes 196616 | tf_op jit(solution)/shard_map/ppermute | solution.py:31
  45.1 0.0 collective-permute-start.2
  45.1 0.6 collective-permute-start.1
  45.6 0.0 copy-start
  45.6 5.3 %shard_map.86 = (bf16[1536,2048]{1,0:T(8,128)(2,1)}, bf16[1536,2048]{1,0:T(8,128)(2,1)}) custom-call(bf16[128,2048]{1,0:T(8,128)(2,1)} %collective-permute-done.after_ref, bf16[128,2048]{1,0:T(8,128)(2,1)} %get-tuple-element.28.last_ref, bf16[128,128,128]{2,1,0:T(8,128)(2,1)} %get-tuple-element.29.lower_ref, ...), custom_call_target="tpu_custom_call", output_to_operand_aliasing={{0}: (5, {}), {1}: (6, {})} | custom-call | flops 67108864 | bytes 3145728 | tf_op jit(solution)/shard_map/pallas_call | solution.py:262
  50.9 0.0 collective-permute-done.3
  50.9 0.0 collective-permute-done.2
  50.9 0.0 collective-permute-done.1
  50.9 0.0 copy-done
  51.0 2.8 %collective-permute-start.6 = (f32[128,128]{1,0:T(8,128)S(1)}, f32[128,128]{1,0:T(8,128)S(1)}, u32[]{:S(2)}, u32[]{:S(2)}) collective-permute-start(f32[128,128]{1,0:T(8,128)S(1)} %add_add_fusion.refs_0_), channel_id=1, source_target_pairs={{0,6},{1,7},{2,4},{3,5},{4,2},{5,3},{6,0},{7,1},{8,14},{9,15},{10,... | collective-permute-start | bytes 196616 | tf_op jit(solution)/shard_map/ppermute | solution.py:31
  53.8 0.5 collective-permute-start.5
  54.3 0.2 collective-permute-start.4
  54.5 0.0 collective-permute-done.7.before_ref
  54.5 4.1 %shard_map.87 = bf16[1536,2048]{1,0:T(8,128)(2,1)} custom-call(bf16[128,2048]{1,0:T(8,128)(2,1)} %collective-permute-done.7.before_ref, bf16[128,2048]{1,0:T(8,128)(2,1)} %get-tuple-element.38.first_ref, bf16[128,128,128]{2,1,0:T(8,128)(2,1)} %get-tuple-element.29.lower_ref, bf16[1536,2048]{1,0:T(8,128)(2,1)} %c_ref.3, ...), custom_call_target="tpu_custom_call", output_to_operand_aliasing={{}: (4, {})} | custom-call | flops 67108864 | bytes 3145728 | tf_op jit(solution)/shard_map/pallas_call | solution.py:262
  58.6 0.0 collective-permute-done.6.refs_3_
  58.6 0.0 collective-permute-done.5.refs_2_
  58.7 0.0 collective-permute-done.4.refs_1_
  58.7 0.1 shard_map.88
  58.8 0.1 collective-permute-start.8
  58.9 1.2 %collective-permute-done.8.refs_2_ = f32[8,128]{1,0:T(8,128)S(1)} collective-permute-done((f32[8,128]{1,0:T(8,128)S(1)}, f32[8,128]{1,0:T(8,128)S(1)}, u32[]{:S(2)}, u32[]{:S(2)}) %collective-permute-start.8) | collective-permute-done | bytes 4128 | tf_op jit(solution)/shard_map/ppermute | solution.py:31
  60.0 0.8 %shard_map.89 = f32[128,128]{1,0:T(8,128)} custom-call(f32[128,128]{1,0:T(8,128)S(1)} %get-tuple-element.46.refs_0_, f32[8,128]{1,0:T(8,128)S(1)} %get-tuple-element.47.refs_1_, f32[8,128]{1,0:T(8,128)S(1)} %collective-permute-done.8.refs_2_), custom_call_target="tpu_custom_call" | custom-call | tf_op jit(solution)/shard_map/pallas_call | solution.py:296
  (1 shorter events, 0.0 us)
Async XLA Ops:
  3.3 32.2 %collective-permute-start = (bf16[128,2048]{1,0:T(8,128)(2,1)}, bf16[128,2048]{1,0:T(8,128)(2,1)}, u32[]{:S(2)}, u32[]{:S(2)}) collective-permute-start(bf16[128,2048]{1,0:T(8,128)(2,1)} %get-tuple-element.26), channel_id=1, source_target_pairs={{4,0},{8,4},{12,8},{16,12},{20,16},{24,20},{28,24},{5,1},{9,5},{13... | collective-permute-start | bytes 1572872 | tf_op jit(solution)/shard_map/ppermute | solution.py:25
  4.5 50.0 %collective-permute-start.7 = (bf16[128,2048]{1,0:T(8,128)(2,1)}, bf16[128,2048]{1,0:T(8,128)(2,1)}, u32[]{:S(2)}, u32[]{:S(2)}) collective-permute-start(bf16[128,2048]{1,0:T(8,128)(2,1)} %get-tuple-element.37), channel_id=1, source_target_pairs={{0,4},{4,8},{8,12},{12,16},{16,20},{20,24},{24,28},{1,5},{5,9},{9,... | collective-permute-start | bytes 1572872 | tf_op jit(solution)/shard_map/ppermute | solution.py:25
  40.9 10.0 %collective-permute-start.3 = (f32[128,128]{1,0:T(8,128)}, f32[128,128]{1,0:T(8,128)S(1)}, u32[]{:S(2)}, u32[]{:S(2)}) collective-permute-start(f32[128,128]{1,0:T(8,128)} %shard_map.85), channel_id=1, source_target_pairs={{0,24},{1,25},{2,26},{3,27},{4,28},{5,29},{6,30},{7,31},{8,16},{9,... | collective-permute-start | bytes 196616 | tf_op jit(solution)/shard_map/ppermute | solution.py:31
  45.1 5.9 %collective-permute-start.2 = (f32[128,128]{1,0:T(8,128)}, f32[128,128]{1,0:T(8,128)S(1)}, u32[]{:S(2)}, u32[]{:S(2)}) collective-permute-start(f32[128,128]{1,0:T(8,128)} %shard_map.85), channel_id=1, source_target_pairs={{0,16},{1,17},{2,18},{3,19},{4,20},{5,21},{6,22},{7,23},{8,24},{9,... | collective-permute-start | bytes 196616 | tf_op jit(solution)/shard_map/ppermute | solution.py:31
  45.1 5.9 %collective-permute-start.1 = (f32[128,128]{1,0:T(8,128)}, f32[128,128]{1,0:T(8,128)S(1)}, u32[]{:S(2)}, u32[]{:S(2)}) collective-permute-start(f32[128,128]{1,0:T(8,128)} %shard_map.85), channel_id=1, source_target_pairs={{0,8},{1,9},{2,10},{3,11},{4,12},{5,13},{6,14},{7,15},{8,0},{9,1},... | collective-permute-start | bytes 196616 | tf_op jit(solution)/shard_map/ppermute | solution.py:31
  45.6 5.3 %copy-start = (f32[128,128]{1,0:T(8,128)S(1)}, f32[128,128]{1,0:T(8,128)}, u32[]{:S(2)}) copy-start(f32[128,128]{1,0:T(8,128)} %shard_map.85) | copy-start | bytes 196612
  51.0 7.7 %collective-permute-start.6 = (f32[128,128]{1,0:T(8,128)S(1)}, f32[128,128]{1,0:T(8,128)S(1)}, u32[]{:S(2)}, u32[]{:S(2)}) collective-permute-start(f32[128,128]{1,0:T(8,128)S(1)} %add_add_fusion.refs_0_), channel_id=1, source_target_pairs={{0,6},{1,7},{2,4},{3,5},{4,2},{5,3},{6,0},{7,1},{8,14},{9,15},{10,... | collective-permute-start | bytes 196616 | tf_op jit(solution)/shard_map/ppermute | solution.py:31
  53.8 4.8 %collective-permute-start.5 = (f32[128,128]{1,0:T(8,128)S(1)}, f32[128,128]{1,0:T(8,128)S(1)}, u32[]{:S(2)}, u32[]{:S(2)}) collective-permute-start(f32[128,128]{1,0:T(8,128)S(1)} %add_add_fusion.refs_0_), channel_id=1, source_target_pairs={{0,2},{1,3},{2,0},{3,1},{4,6},{5,7},{6,4},{7,5},{8,10},{9,11},{10,... | collective-permute-start | bytes 196616 | tf_op jit(solution)/shard_map/ppermute | solution.py:31
  54.3 4.3 %collective-permute-start.4 = (f32[128,128]{1,0:T(8,128)S(1)}, f32[128,128]{1,0:T(8,128)S(1)}, u32[]{:S(2)}, u32[]{:S(2)}) collective-permute-start(f32[128,128]{1,0:T(8,128)S(1)} %add_add_fusion.refs_0_), channel_id=1, source_target_pairs={{0,4},{1,5},{2,6},{3,7},{4,0},{5,1},{6,2},{7,3},{8,12},{9,13},{10,... | collective-permute-start | bytes 196616 | tf_op jit(solution)/shard_map/ppermute | solution.py:31
  58.8 1.2 %collective-permute-start.8 = (f32[8,128]{1,0:T(8,128)S(1)}, f32[8,128]{1,0:T(8,128)S(1)}, u32[]{:S(2)}, u32[]{:S(2)}) collective-permute-start(f32[8,128]{1,0:T(8,128)S(1)} %get-tuple-element.47.refs_1_), channel_id=1, source_target_pairs={{0,1},{1,0},{2,3},{3,2},{4,5},{5,4},{6,7},{7,6},{8,9},{9,8},{10,11... | collective-permute-start | bytes 12296 | tf_op jit(solution)/shard_map/ppermute | solution.py:31
